TPU v7x, 128 devices: a whole 4x4x4 slice. The times are simulated.
128 devices in a mesh: ctx: 32 (over y, z, x_hi), tp: 4 (over x_lo, core).
Axes of the slice: x: 4 (x_hi: 2, x_lo: 2; x = x_hi * 2 + x_lo), y: 4, z: 4, core: 2. Of those that a mesh axis runs over, the one named last changes fastest.
Arguments:
- kv_product: bfloat16 [2048, 32768], P('tp', 'ctx'), may hold values from -6 to 6
- query: bfloat16 [2048, 32768], P('tp', 'ctx'), may hold values from -6 to 6
- decay_rate: float32 [2048, 16], P('tp'), as said below
- residue: float32 [2048, 16], P('tp'), may hold values from -1.5 to 1.5
- out_weight: bfloat16 [2048, 2048], P('tp'), may hold values from -0.125 to 0.125
Outputs:
- output: bfloat16 [32768, 2048], P(('ctx', 'tp'))
Inputs may be any that keep to these rules, and one draw needn't show every extreme that they name: `decay_rate`: every rate is positive and at most 0.08.
All inputs are finite; a program needn't handle non-finite values.
Results may differ from a plain program's by a relative error of at most 0.0058.
Values may be sent and summed in bfloat16 or wider, within the bound.
A program may use at most 128 MiB of HBM per device.

v0:
```python
import jax
import jax.numpy as jnp
from jax import lax
from jax.experimental import pallas as pl
from jax.experimental.pallas import tpu as pltpu
from jax.sharding import PartitionSpec as P

NY, NZ, NX, NTP = 4, 4, 2, 4
SUBS, LANES = 8, 128
W_PIECES, W_DIRECT = 8, 3
MESH = pl.DeviceIdType.MESH


def one_minus_exp(z):
    series = jnp.ones_like(z)
    for n in range(10, 1, -1):
        series = 1.0 - (z * (1.0 / n)) * series
    return jnp.where(z < 0.5, z * series, 1.0 - jnp.exp(-z))


def shift_rows(value, by, row):
    return jnp.where(row >= by, pltpu.roll(value, by, 0), 0.0)


def kernel(
    kv_hbm, q_hbm, dec_hbm, res_hbm, w_hbm, out_ref,
    kv_v, q_v, dec_v, res_v, wf, xs, qs, ys, dec_t, lam_t, wgt_t, wc_t, ends,
    s_own, s_x, g_z, h_y, inc, gb, gin, acc,
    loc_sem, x_sem, z_send, z_recv, y_send, y_recv,
    wsib_sem, wp_send, wp_recv, wf_send, wf_recv, g_send, g_recv,
):
    chans, toks = kv_v.shape
    modes = dec_v.shape[1]
    groups = chans // LANES
    sub_len = toks // SUBS
    out_toks, cols = out_ref.shape
    seq = float(toks * NY * NZ * NX)

    ctx, tp = lax.axis_index("ctx"), lax.axis_index("tp")
    x_hi = lax.rem(ctx, NX)
    z = lax.rem(ctx // NX, NZ)
    y = ctx // (NX * NZ)
    x_lo, core = tp // 2, lax.rem(tp, 2)

    def ctx_of(yy, zz, xx):
        return (yy * NZ + zz) * NX + xx

    partner_tp = [tp, x_lo * 2 + (1 - core), (1 - x_lo) * 2 + core, (1 - x_lo) * 2 + (1 - core)]
    to_x = {"ctx": ctx_of(y, z, 1 - x_hi), "tp": tp}
    to_z = [{"ctx": ctx_of(y, lax.rem(z + j, NZ), x_hi), "tp": tp} for j in range(NZ)]
    to_y = [{"ctx": ctx_of(lax.rem(y + j, NY), z, x_hi), "tp": tp} for j in range(NY)]
    to_tp = [{"ctx": ctx, "tp": t} for t in partner_tp]
    to_wrap = {"ctx": ctx_of(y, z, 1 - x_hi), "tp": partner_tp[2]}

    loads = [
        pltpu.make_async_copy(dec_hbm, dec_v, loc_sem.at[0]),
        pltpu.make_async_copy(res_hbm, res_v, loc_sem.at[1]),
        pltpu.make_async_copy(kv_hbm, kv_v, loc_sem.at[2]),
        pltpu.make_async_copy(q_hbm, q_v, loc_sem.at[3]),
        pltpu.make_async_copy(w_hbm, wf.at[0], loc_sem.at[4]),
    ]
    for load in loads:
        load.start()

    barrier = pltpu.get_barrier_semaphore()
    partners = [to_x] + to_z[1:] + to_y[1:] + to_tp[1:] + [to_wrap]
    for partner in partners:
        pl.semaphore_signal(barrier, inc=1, device_id=partner, device_id_type=MESH)
    pl.semaphore_wait(barrier, len(partners))

    def remote(src, dst, send, recv, to):
        return pltpu.make_async_remote_copy(
            src_ref=src, dst_ref=dst, send_sem=send, recv_sem=recv, device_id=to, device_id_type=MESH
        )

    w_sib = remote(w_hbm, wf.at[1], wsib_sem.at[0], wsib_sem.at[1], to_tp[1])
    w_rows = chans // W_PIECES
    w_cross, w_fwd = [], []
    for p in range(W_PIECES):
        rows = pl.ds(p * w_rows, w_rows)
        to = to_tp[2] if p < W_DIRECT else to_wrap
        w_cross.append(remote(w_hbm.at[rows], wf.at[2, rows], wp_send.at[p], wp_recv.at[p], to))
        w_fwd.append(remote(wf.at[2, rows], wf.at[3, rows], wf_send.at[p], wf_recv.at[p], to_tp[1]))
    w_order = []
    for i in range(W_PIECES):
        for p in (W_DIRECT + i, i):
            if (p < W_DIRECT if p == i else p < W_PIECES):
                w_order.append(p)
    for p in w_order:
        w_cross[p].start()
    w_sib.start()

    loads[0].wait()
    loads[1].wait()
    for g in range(groups):
        rows = slice(g * LANES, (g + 1) * LANES)
        dec = dec_v[rows, :].T
        res = res_v[rows, :].T
        wgt = res * jnp.sqrt(one_minus_exp(2.0 * dec))
        dec_t[g] = dec
        lam_t[g] = jnp.exp(-dec)
        wgt_t[g] = wgt
        wc_t[g] = wgt * one_minus_exp(seq * dec)

    tile = 2 * LANES
    eye = (
        lax.broadcasted_iota(jnp.int32, (tile, tile), 0) == lax.broadcasted_iota(jnp.int32, (tile, tile), 1)
    ).astype(jnp.bfloat16)

    def turn(src, dst):
        for cb in range(chans // tile):
            for tb in range(toks // tile):
                block = src[cb * tile:(cb + 1) * tile, tb * tile:(tb + 1) * tile]
                turned = lax.dot_general(
                    eye, block, (((1,), (1,)), ((), ())), preferred_element_type=jnp.float32
                )
                dst[2 * cb, tb * tile:(tb + 1) * tile, :] = turned[:, :LANES]
                dst[2 * cb + 1, tb * tile:(tb + 1) * tile, :] = turned[:, LANES:]

    loads[2].wait()
    turn(kv_v, xs)

    row = lax.broadcasted_iota(jnp.int32, (SUBS, LANES), 0)
    left = (SUBS - 1 - row).astype(jnp.float32) * float(sub_len)

    def wide(ref, g, m):
        return jnp.broadcast_to(ref[g, m:m + 1, :], (SUBS, LANES))

    def first_pass(g, carry):
        lam = [wide(lam_t, g, m) for m in range(modes)]

        def step(t, states):
            x = xs[g, pl.ds(t, SUBS, stride=sub_len), :]
            return tuple(l * u + x for l, u in zip(lam, states))

        states = lax.fori_loop(
            0, sub_len, step, tuple(jnp.zeros((SUBS, LANES), jnp.float32) for _ in range(modes)), unroll=8
        )
        for m in range(modes):
            ends[g, m] = states[m]
            decayed = states[m] * jnp.exp(-wide(dec_t, g, m) * left)
            s_own[g, m:m + 1, :] = jnp.sum(decayed, axis=0, keepdims=True)
        return carry

    lax.fori_loop(0, groups, first_pass, 0)

    block = float(toks)
    send_x = remote(s_own, s_x, x_sem.at[0], x_sem.at[1], to_x)
    send_x.start()
    loads[3].wait()
    turn(q_v, qs)
    send_x.wait_recv()
    dec = dec_t[...]
    lam1 = jnp.exp(-block * dec)
    mine, other = s_own[...], s_x[...]
    g_z[0] = jnp.where(x_hi == 0, other + lam1 * mine, mine + lam1 * other)
    sends_z = [remote(g_z.at[0], g_z.at[j], z_send.at[j], z_recv.at[j], to_z[j]) for j in range(1, NZ)]
    for send in sends_z:
        send.start()
    for send in sends_z:
        send.wait_recv()
    total = jnp.zeros_like(dec)
    before = jnp.zeros_like(dec)
    for j in range(NZ):
        part = g_z[j]
        after = (NZ - 1 - lax.rem(z + NZ - j, NZ)).astype(jnp.float32) * (block * NX)
        total += jnp.exp(-after * dec) * part
        if j:
            before += jnp.where(z >= j, jnp.exp(-(block * NX * (j - 1)) * dec) * part, 0.0)
    h_y[0] = total
    sends_y = [remote(h_y.at[0], h_y.at[j], y_send.at[j], y_recv.at[j], to_y[j]) for j in range(1, NY)]
    for send in sends_y:
        send.start()
    for send in sends_y:
        send.wait_recv()
    came = jnp.zeros_like(dec)
    for j in range(1, NY + 1):
        came += jnp.exp(-(block * NX * NZ * (j - 1)) * dec) * h_y[j % NY]
    once = one_minus_exp(seq * dec)
    came = jnp.exp(-(z.astype(jnp.float32) * (block * NX)) * dec) * came + once * before
    inc[...] = jnp.where(x_hi == 0, came, lam1 * came + once * other)

    g_sends = [
        [
            remote(
                gb.at[g, pl.ds(pl.multiple_of(partner_tp[r] * out_toks, out_toks), out_toks)],
                gin.at[r - 1, g], g_send.at[r - 1, g], g_recv.at[r - 1, g], to_tp[r],
            )
            for r in range(1, NTP)
        ]
        for g in range(groups)
    ]
    for g in range(groups):
        start = []
        for m in range(modes):
            decs = wide(dec_t, g, m)
            state = jnp.where(row == 0, wide(inc, g, m), 0.0)
            state += shift_rows(ends[g, m] * one_minus_exp(seq * decs), 1, row)
            for by in (1, 2, 4):
                state += jnp.exp(-float(by * sub_len) * decs) * shift_rows(state, by, row)
            start.append(wide(wgt_t, g, m) * state)
        lam = [wide(lam_t, g, m) for m in range(modes)]
        gain = [wide(wc_t, g, m) for m in range(modes)]

        def step(t, states):
            x = xs[g, pl.ds(t, SUBS, stride=sub_len), :]
            states = tuple(l * u + c * x for l, u, c in zip(lam, states, gain))
            level = list(states)
            while len(level) > 1:
                level = [a + b for a, b in zip(level[::2], level[1::2])]
            ys[g, pl.ds(t, SUBS, stride=sub_len), :] = level[0]
            return states

        lax.fori_loop(0, sub_len, step, tuple(start), unroll=4)
        conv = ys[g].astype(jnp.bfloat16).astype(jnp.float32)
        gb[g] = (qs[g] * conv).astype(jnp.bfloat16)
        for send in (g_sends[g][1], g_sends[g][2], g_sends[g][0]):
            send.start()

    n_tile = 512

    def project(r, lhs_of, last):
        lhs = jnp.concatenate([lhs_of(g) for g in range(groups)], axis=1)

        def body(n, carry):
            at = pl.ds(pl.multiple_of(n * n_tile, n_tile), n_tile)
            part = jnp.dot(lhs, wf[r, :, at], preferred_element_type=jnp.float32)
            if r > 0:
                part += acc[:, at]
            if last:
                out_ref[:, at] = part.astype(jnp.bfloat16)
            else:
                acc[:, at] = part
            return carry

        lax.fori_loop(0, cols // n_tile, body, 0)

    loads[4].wait()
    own_rows = pl.ds(pl.multiple_of(tp * out_toks, out_toks), out_toks)
    project(0, lambda g: gb[g, own_rows, :], False)
    for p in w_order:
        w_cross[p].wait_recv()
        w_fwd[p].start()
    w_sib.wait_recv()
    for g in range(groups):
        g_sends[g][0].wait_recv()
    project(1, lambda g: gin[0, g], False)
    for g in range(groups):
        g_sends[g][1].wait_recv()
    project(2, lambda g: gin[1, g], False)
    for p in w_order:
        w_fwd[p].wait_recv()
    for g in range(groups):
        g_sends[g][2].wait_recv()
    project(3, lambda g: gin[2, g], True)

    w_sib.wait_send()
    send_x.wait_send()
    for send in sends_z + sends_y + w_cross + w_fwd:
        send.wait_send()
    for per_group in g_sends:
        for send in per_group:
            send.wait_send()


def shards(kv_product, query, decay_rate, residue, out_weight):
    chans, toks = kv_product.shape
    modes = decay_rate.shape[1]
    cols = out_weight.shape[1]
    groups = chans // LANES
    out_toks = toks // NTP
    bf16, f32 = jnp.bfloat16, jnp.float32
    small = (groups, modes, LANES)
    dma = pltpu.SemaphoreType.DMA
    return pl.pallas_call(
        kernel,
        out_shape=jax.ShapeDtypeStruct((out_toks, cols), bf16),
        in_specs=[pl.BlockSpec(memory_space=pl.ANY)] * 5,
        out_specs=pl.BlockSpec(memory_space=pltpu.VMEM),
        scratch_shapes=[
            pltpu.VMEM((chans, toks), bf16),
            pltpu.VMEM((chans, toks), bf16),
            pltpu.VMEM((chans, modes), f32),
            pltpu.VMEM((chans, modes), f32),
            pltpu.VMEM((NTP, chans, cols), bf16),
            pltpu.VMEM((groups, toks, LANES), f32),
            pltpu.VMEM((groups, toks, LANES), f32),
            pltpu.VMEM((groups, toks, LANES), f32),
            pltpu.VMEM(small, f32),
            pltpu.VMEM(small, f32),
            pltpu.VMEM(small, f32),
            pltpu.VMEM(small, f32),
            pltpu.VMEM((groups, modes, SUBS, LANES), f32),
            pltpu.VMEM(small, f32),
            pltpu.VMEM(small, f32),
            pltpu.VMEM((NZ,) + small, f32),
            pltpu.VMEM((NY,) + small, f32),
            pltpu.VMEM(small, f32),
            pltpu.VMEM((groups, toks, LANES), bf16),
            pltpu.VMEM((NTP - 1, groups, out_toks, LANES), bf16),
            pltpu.VMEM((out_toks, cols), f32),
            dma((5,)),
            dma((2,)),
            dma((NZ,)),
            dma((NZ,)),
            dma((NY,)),
            dma((NY,)),
            dma((2,)),
            dma((W_PIECES,)),
            dma((W_PIECES,)),
            dma((W_PIECES,)),
            dma((W_PIECES,)),
            dma((NTP - 1, groups)),
            dma((NTP - 1, groups)),
        ],
        compiler_params=pltpu.CompilerParams(
            collective_id=0, has_side_effects=True, vmem_limit_bytes=48 * 1024 * 1024
        ),
        cost_estimate=pl.CostEstimate(
            flops=2 * out_toks * cols * chans * NTP, bytes_accessed=6 * 1024 * 1024, transcendentals=0
        ),
    )(kv_product, query, decay_rate, residue, out_weight)


def solution(mesh):
    in_specs = (P("tp", "ctx"), P("tp", "ctx"), P("tp", None), P("tp", None), P("tp", None))
    out_specs = P(("ctx", "tp"), None)
    return jax.shard_map(shards, mesh=mesh, in_specs=in_specs, out_specs=out_specs, check_vma=False)
```

profile of v0, /device:TPU:1, one launch (start us, length us, event | category | flops | bytes accessed | tf_op | source)
XLA Modules:
  0.0 57.4 jit_solution(3237260153452480708)
XLA Ops:
  0.0 0.9 %copy.6.dec_hbm = f32[512,16]{1,0:T(8,128)S(1)} copy(f32[512,16]{0,1:T(8,128)} %param.7) | data formatting | bytes 65536 | tf_op args[2]
  0.9 0.9 %copy.7.res_hbm = f32[512,16]{1,0:T(8,128)S(1)} copy(f32[512,16]{0,1:T(8,128)} %param.8) | data formatting | bytes 65536 | tf_op args[3]
  1.8 0.0 copy-start
  1.8 1.6 %copy-done = bf16[512,2048]{1,0:T(8,128)(2,1)S(1)} copy-done((bf16[512,2048]{1,0:T(8,128)(2,1)S(1)}, bf16[512,2048]{1,0:T(8,128)(2,1)}, u32[]{:S(2)}) %copy-start) | copy-done | bytes 2097176
  3.4 0.0 copy-start.1
  3.4 1.2 %copy-done.1 = bf16[512,1024]{1,0:T(8,128)(2,1)S(1)} copy-done((bf16[512,1024]{1,0:T(8,128)(2,1)S(1)}, bf16[512,1024]{1,0:T(8,128)(2,1)}, u32[]{:S(2)}) %copy-start.1) | copy-done | bytes 1048600
  4.6 0.0 copy-start.2
  4.6 1.2 %copy-done.2 = bf16[512,1024]{1,0:T(8,128)(2,1)S(1)} copy-done((bf16[512,1024]{1,0:T(8,128)(2,1)S(1)}, bf16[512,1024]{1,0:T(8,128)(2,1)}, u32[]{:S(2)}) %copy-start.2) | copy-done | bytes 1048600
  5.8 50.6 %shard_map.55 = bf16[256,2048]{1,0:T(8,128)(2,1)S(1)} custom-call(bf16[512,1024]{1,0:T(8,128)(2,1)S(1)} %copy-done.1, bf16[512,1024]{1,0:T(8,128)(2,1)S(1)} %copy-done.2, f32[512,16]{1,0:T(8,128)S(1)} %copy.6.dec_hbm, f32[512,16]{1,0:T(8,128)S(1)} %copy.7.res_hbm, bf16[512,2048]{1,0:T(8,128)(2,1)S(1)} %copy-done), custom_call_target="tpu_custom_call" | custom-call | flops 2147483648 | bytes 6291456 | tf_op jit(solution)/shard_map/pallas_call | solution.py:275
  56.4 1.0 %copy.9 = bf16[256,2048]{1,0:T(8,128)(2,1)} copy(bf16[256,2048]{1,0:T(8,128)(2,1)S(1)} %shard_map.55) | data formatting | bytes 2097152
Async XLA Ops:
  1.8 1.6 %copy-start = (bf16[512,2048]{1,0:T(8,128)(2,1)S(1)}, bf16[512,2048]{1,0:T(8,128)(2,1)}, u32[]{:S(2)}) copy-start(bf16[512,2048]{1,0:T(8,128)(2,1)} %w_hbm.1) | copy-start | bytes 6291460
  3.4 1.2 %copy-start.1 = (bf16[512,1024]{1,0:T(8,128)(2,1)S(1)}, bf16[512,1024]{1,0:T(8,128)(2,1)}, u32[]{:S(2)}) copy-start(bf16[512,1024]{1,0:T(8,128)(2,1)} %kv_hbm.1) | copy-start | bytes 3145732
  4.6 1.2 %copy-start.2 = (bf16[512,1024]{1,0:T(8,128)(2,1)S(1)}, bf16[512,1024]{1,0:T(8,128)(2,1)}, u32[]{:S(2)}) copy-start(bf16[512,1024]{1,0:T(8,128)(2,1)} %q_hbm.1) | copy-start | bytes 3145732
where the time goes:
time: 57.7 us; the launch traced here: 57.4 us
  Pallas kernels  50.6 us (88%)
  local copies, waits for them, and re-layouts  6.77 us (12%)
    pallas_call x1, Pallas kernels, shards(): pl.pallas_call(kernel, out_shape=jax.ShapeDtypeStruct((out_toks, cols), b...  50.6 us
    unnamed x9, local copies, waits for them, and re-layouts  6.77 us

commit v1 on v0

v1 whole, which is shorter than its diff:
```python
import jax
import jax.numpy as jnp
from jax import lax
from jax.experimental import pallas as pl
from jax.experimental.pallas import tpu as pltpu
from jax.sharding import PartitionSpec as P

NY, NZ, NX, NTP = 4, 4, 2, 4
SUBS, LANES = 8, 128
W_IMPORT = ("wrap", "direct", "wrap", "direct", "wrap", "direct", "wrap", "wrap")
UNROLL = 16
MESH = pl.DeviceIdType.MESH


def one_minus_exp(z):
    series = jnp.ones_like(z)
    for n in range(10, 1, -1):
        series = 1.0 - (z * (1.0 / n)) * series
    return jnp.where(z < 0.5, z * series, 1.0 - jnp.exp(-z))


def shift_rows(value, by, row):
    return jnp.where(row >= by, pltpu.roll(value, by, 0), 0.0)


def tree_sum(terms):
    while len(terms) > 1:
        terms = [a + b for a, b in zip(terms[::2], terms[1::2])]
    return terms[0]


def kernel(
    kv_hbm, q_hbm, dec_hbm, res_hbm, w_hbm, out_ref,
    kv_v, q_v, dec_v, res_v, wf, xs, qs, ys, yn, dec_t, lam_t, wgt_t, wc_t, ends,
    s_own, s_x, g_z, h_y, inc, gb, gin, acc,
    loc_sem, x_sem, z_send, z_recv, y_send, y_recv,
    wsib_sem, wi_send, wi_recv, wn_send, wn_recv, wf_send, wf_recv, g_send, g_recv,
):
    chans, toks = kv_v.shape
    modes = dec_v.shape[0]
    groups = chans // LANES
    sub_len = toks // SUBS
    out_toks, cols = out_ref.shape
    seq = float(toks * NY * NZ * NX)

    ctx, tp = lax.axis_index("ctx"), lax.axis_index("tp")
    x_hi = lax.rem(ctx, NX)
    z = lax.rem(ctx // NX, NZ)
    y = ctx // (NX * NZ)
    x_lo, core = tp // 2, lax.rem(tp, 2)

    def ctx_of(yy, zz, xx):
        return (yy * NZ + zz) * NX + xx

    partner_tp = [tp, x_lo * 2 + (1 - core), (1 - x_lo) * 2 + core, (1 - x_lo) * 2 + (1 - core)]
    to_x = {"ctx": ctx_of(y, z, 1 - x_hi), "tp": tp}
    to_z = [{"ctx": ctx_of(y, lax.rem(z + j, NZ), x_hi), "tp": tp} for j in range(NZ)]
    to_y = [{"ctx": ctx_of(lax.rem(y + j, NY), z, x_hi), "tp": tp} for j in range(NY)]
    to_tp = [{"ctx": ctx, "tp": t} for t in partner_tp]
    to_wrap = {"ctx": ctx_of(y, z, 1 - x_hi), "tp": partner_tp[2]}

    loads = [
        pltpu.make_async_copy(kv_hbm, kv_v, loc_sem.at[0]),
        pltpu.make_async_copy(dec_hbm, dec_v, loc_sem.at[1]),
        pltpu.make_async_copy(res_hbm, res_v, loc_sem.at[2]),
        pltpu.make_async_copy(q_hbm, q_v, loc_sem.at[3]),
        pltpu.make_async_copy(w_hbm, wf.at[0], loc_sem.at[4]),
    ]
    for load in loads:
        load.start()

    barrier = pltpu.get_barrier_semaphore()
    partners = [to_x] + to_z[1:] + to_y[1:] + to_tp[1:] + [to_wrap]
    for partner in partners:
        pl.semaphore_signal(barrier, inc=1, device_id=partner, device_id_type=MESH)

    loads[1].wait()
    loads[2].wait()
    for g in range(groups):
        lanes = slice(g * LANES, (g + 1) * LANES)
        dec = dec_v[:, lanes]
        wgt = res_v[:, lanes] * jnp.sqrt(one_minus_exp(2.0 * dec))
        dec_t[g] = dec
        lam_t[g] = jnp.exp(-dec)
        wgt_t[g] = wgt
        wc_t[g] = wgt * one_minus_exp(seq * dec)

    def turn(src, dst, runs):
        for g in range(groups):
            for s in range(SUBS):
                turned = src[g * LANES:(g + 1) * LANES, s * sub_len:(s + 1) * sub_len].T.astype(jnp.float32)
                if runs:
                    dst[g, pl.ds(s, sub_len, stride=SUBS), :] = turned
                else:
                    dst[g, s * sub_len:(s + 1) * sub_len, :] = turned

    loads[0].wait()
    turn(kv_v, xs, True)

    pl.semaphore_wait(barrier, len(partners))

    def remote(src, dst, send, recv, to):
        return pltpu.make_async_remote_copy(
            src_ref=src, dst_ref=dst, send_sem=send, recv_sem=recv, device_id=to, device_id_type=MESH
        )

    half = chans // 2
    parity = lax.rem(y + z, 2)
    pieces = len(W_IMPORT)
    rows_in = half // pieces

    def rows_of(which, p):
        return pl.ds(pl.multiple_of(which * half + p * rows_in, rows_in), rows_in)

    around = [to_y[1], to_y[NY - 1], to_z[1], to_z[NZ - 1]]
    w_sib = remote(w_hbm, wf.at[1], wsib_sem.at[0], wsib_sem.at[1], to_tp[1])
    w_import, w_near, w_across = [], [], []
    for p in range(pieces):
        rows = rows_of(parity, p)
        to = to_wrap if W_IMPORT[p] == "wrap" else to_tp[2]
        w_import.append(remote(w_hbm.at[rows], wf.at[2, rows], wi_send.at[p], wi_recv.at[p], to))
        w_near.append(remote(wf.at[2, rows], wf.at[2, rows], wn_send.at[p], wn_recv.at[p], around[p % 4]))
        w_across.append(remote(wf.at[2, rows], wf.at[3, rows], wf_send.at[p], wf_recv.at[p], to_tp[1]))
    w_got = []
    for p in range(pieces):
        rows = rows_of(1 - parity, p)
        w_got.append(remote(wf.at[2, rows], wf.at[2, rows], wn_send.at[p], wn_recv.at[p], around[p % 4]))
        w_across.append(
            remote(wf.at[2, rows], wf.at[3, rows], wf_send.at[pieces + p], wf_recv.at[pieces + p], to_tp[1])
        )
    for copy in w_import:
        copy.start()
    w_sib.start()

    def hand_on(*which):
        for p in which:
            w_import[p].wait_recv()
            w_near[p].start()
            w_across[p].start()

    row = lax.broadcasted_iota(jnp.int32, (SUBS, LANES), 0)
    left = (SUBS - 1 - row).astype(jnp.float32) * float(sub_len)

    def wide(ref, g, m):
        return jnp.broadcast_to(ref[g, m:m + 1, :], (SUBS, LANES))

    def at(t):
        return pl.ds(pl.multiple_of(t * SUBS, SUBS), SUBS)

    zeros = tuple(jnp.zeros((SUBS, LANES), jnp.float32) for _ in range(modes))

    def first_pass(g, carry):
        lam = [wide(lam_t, g, m) for m in range(modes)]

        def step(t, states):
            x = xs[g, at(t), :]
            return tuple(l * u + x for l, u in zip(lam, states))

        states = lax.fori_loop(0, sub_len, step, zeros, unroll=UNROLL)
        for m in range(modes):
            ends[g, m] = states[m]
            decayed = states[m] * jnp.exp(-wide(dec_t, g, m) * left)
            s_own[g, m:m + 1, :] = jnp.sum(decayed, axis=0, keepdims=True)
        return carry

    lax.fori_loop(0, groups, first_pass, 0)

    def second_pass(g):
        lam = [wide(lam_t, g, m) for m in range(modes)]
        gain = [wide(wc_t, g, m) for m in range(modes)]

        def step(t, states):
            x = xs[g, at(t), :]
            states = tuple(l * u + x for l, u in zip(lam, states))
            ys[g, at(t), :] = tree_sum([c * u for c, u in zip(gain, states)])
            return states

        lax.fori_loop(0, sub_len, step, zeros, unroll=UNROLL)

    block = float(toks)
    send_x = remote(s_own, s_x, x_sem.at[0], x_sem.at[1], to_x)
    send_x.start()
    loads[3].wait()
    turn(q_v, qs, False)
    second_pass(0)
    hand_on(0, 1)
    second_pass(1)
    send_x.wait_recv()
    dec = dec_t[...]
    lam1 = jnp.exp(-block * dec)
    mine, other = s_own[...], s_x[...]
    g_z[0] = jnp.where(x_hi == 0, other + lam1 * mine, mine + lam1 * other)
    sends_z = [remote(g_z.at[0], g_z.at[j], z_send.at[j], z_recv.at[j], to_z[j]) for j in range(1, NZ)]
    for send in sends_z:
        send.start()
    hand_on(2, 3)
    second_pass(2)
    hand_on(4, 5)
    second_pass(3)
    for send in sends_z:
        send.wait_recv()
    total = jnp.zeros_like(dec)
    before = jnp.zeros_like(dec)
    for j in range(NZ):
        part = g_z[j]
        after = (NZ - 1 - lax.rem(z + NZ - j, NZ)).astype(jnp.float32) * (block * NX)
        total += jnp.exp(-after * dec) * part
        if j:
            before += jnp.where(z >= j, jnp.exp(-(block * NX * (j - 1)) * dec) * part, 0.0)
    h_y[0] = total
    sends_y = [remote(h_y.at[0], h_y.at[j], y_send.at[j], y_recv.at[j], to_y[j]) for j in range(1, NY)]
    for send in sends_y:
        send.start()
    hand_on(6, 7)
    for send in sends_y:
        send.wait_recv()
    came = jnp.zeros_like(dec)
    for j in range(1, NY + 1):
        came += jnp.exp(-(block * NX * NZ * (j - 1)) * dec) * h_y[j % NY]
    once = one_minus_exp(seq * dec)
    came = jnp.exp(-(z.astype(jnp.float32) * (block * NX)) * dec) * came + once * before
    inc[...] = jnp.where(x_hi == 0, came, lam1 * came + once * other)

    g_sends = [
        [
            remote(
                gb.at[g, pl.ds(pl.multiple_of(partner_tp[r] * out_toks, out_toks), out_toks)],
                gin.at[r - 1, g], g_send.at[r - 1, g], g_recv.at[r - 1, g], to_tp[r],
            )
            for r in range(1, NTP)
        ]
        for g in range(groups)
    ]
    for g in range(groups):
        start = []
        for m in range(modes):
            decs = wide(dec_t, g, m)
            state = jnp.where(row == 0, wide(inc, g, m), 0.0)
            state += shift_rows(ends[g, m] * one_minus_exp(seq * decs), 1, row)
            for by in (1, 2, 4):
                state += jnp.exp(-float(by * sub_len) * decs) * shift_rows(state, by, row)
            start.append(wide(wgt_t, g, m) * state)
        lam = [wide(lam_t, g, m) for m in range(modes)]

        def step(t, states):
            states = tuple(l * u for l, u in zip(lam, states))
            yn[g, pl.ds(t, SUBS, stride=sub_len), :] = ys[g, at(t), :] + tree_sum(list(states))
            return states

        lax.fori_loop(0, sub_len, step, tuple(start), unroll=UNROLL)
        conv = yn[g].astype(jnp.bfloat16).astype(jnp.float32)
        gb[g] = (qs[g] * conv).astype(jnp.bfloat16)
        for send in (g_sends[g][1], g_sends[g][2], g_sends[g][0]):
            send.start()

    for p in range(pieces):
        w_got[p].wait_recv()
        w_across[pieces + p].start()

    own_rows = pl.ds(pl.multiple_of(tp * out_toks, out_toks), out_toks)
    loads[4].wait()
    w_sib.wait_recv()
    for g in range(groups):
        g_sends[g][0].wait_recv()
    lhs = jnp.concatenate(
        [gb[g, own_rows, :] for g in range(groups)] + [gin[0, g] for g in range(groups)], axis=1
    )
    acc[...] = jnp.dot(
        lhs, jnp.concatenate([wf[0], wf[1]], axis=0), preferred_element_type=jnp.float32
    )
    for copy in w_across:
        copy.wait_recv()
    for g in range(groups):
        rows = slice(g * LANES, (g + 1) * LANES)
        g_sends[g][1].wait_recv()
        g_sends[g][2].wait_recv()
        lhs = jnp.concatenate([gin[1, g], gin[2, g]], axis=1)
        rhs = jnp.concatenate([wf[2, rows, :], wf[3, rows, :]], axis=0)
        part = acc[...] + jnp.dot(lhs, rhs, preferred_element_type=jnp.float32)
        if g == groups - 1:
            out_ref[...] = part.astype(jnp.bfloat16)
        else:
            acc[...] = part

    for copy in [w_sib, send_x] + sends_z + sends_y + w_import + w_near + w_across:
        copy.wait_send()
    for per_group in g_sends:
        for send in per_group:
            send.wait_send()


def shards(kv_product, query, decay_rate, residue, out_weight):
    chans, toks = kv_product.shape
    modes = decay_rate.shape[1]
    cols = out_weight.shape[1]
    groups = chans // LANES
    out_toks = toks // NTP
    pieces = len(W_IMPORT)
    bf16, f32 = jnp.bfloat16, jnp.float32
    small = (groups, modes, LANES)
    dma = pltpu.SemaphoreType.DMA
    return pl.pallas_call(
        kernel,
        out_shape=jax.ShapeDtypeStruct((out_toks, cols), bf16),
        in_specs=[pl.BlockSpec(memory_space=pltpu.HBM)] * 5,
        out_specs=pl.BlockSpec(memory_space=pltpu.VMEM),
        scratch_shapes=[
            pltpu.VMEM((chans, toks), bf16),
            pltpu.VMEM((chans, toks), bf16),
            pltpu.VMEM((modes, chans), f32),
            pltpu.VMEM((modes, chans), f32),
            pltpu.VMEM((NTP, chans, cols), bf16),
            pltpu.VMEM((groups, toks, LANES), f32),
            pltpu.VMEM((groups, toks, LANES), f32),
            pltpu.VMEM((groups, toks, LANES), f32),
            pltpu.VMEM((groups, toks, LANES), f32),
            pltpu.VMEM(small, f32),
            pltpu.VMEM(small, f32),
            pltpu.VMEM(small, f32),
            pltpu.VMEM(small, f32),
            pltpu.VMEM((groups, modes, SUBS, LANES), f32),
            pltpu.VMEM(small, f32),
            pltpu.VMEM(small, f32),
            pltpu.VMEM((NZ,) + small, f32),
            pltpu.VMEM((NY,) + small, f32),
            pltpu.VMEM(small, f32),
            pltpu.VMEM((groups, toks, LANES), bf16),
            pltpu.VMEM((NTP - 1, groups, out_toks, LANES), bf16),
            pltpu.VMEM((out_toks, cols), f32),
            dma((5,)),
            dma((2,)),
            dma((NZ,)),
            dma((NZ,)),
            dma((NY,)),
            dma((NY,)),
            dma((2,)),
            dma((pieces,)),
            dma((pieces,)),
            dma((pieces,)),
            dma((pieces,)),
            dma((2 * pieces,)),
            dma((2 * pieces,)),
            dma((NTP - 1, groups)),
            dma((NTP - 1, groups)),
        ],
        compiler_params=pltpu.CompilerParams(
            collective_id=0, has_side_effects=True, vmem_limit_bytes=52 * 1024 * 1024
        ),
        cost_estimate=pl.CostEstimate(
            flops=2 * out_toks * cols * chans * NTP, bytes_accessed=6 * 1024 * 1024, transcendentals=0
        ),
    )(kv_product, query, decay_rate.T, residue.T, out_weight)


def solution(mesh):
    in_specs = (P("tp", "ctx"), P("tp", "ctx"), P("tp", None), P("tp", None), P("tp", None))
    out_specs = P(("ctx", "tp"), None)
    return jax.shard_map(shards, mesh=mesh, in_specs=in_specs, out_specs=out_specs, check_vma=False)
```

time: 57.7 us -> 43 us (0.75)
  Pallas kernels: 50.6 us -> 40.3 us
  local copies, waits for them, and re-layouts: 6.77 us -> 2.49 us
    pallas_call x1, Pallas kernels: 50.6 us -> 40.3 us  [shards(): pl.pallas_call(kernel, out_shape=jax.ShapeDtypeStruct((out_toks, cols), b...]
    unnamed x9 -> x5, local copies, waits for them, and re-layouts: 6.77 us -> 2.49 us
where the time goes in v1:
time: 43 us; the launch traced here: 42.8 us
  Pallas kernels  40.3 us (94%)
  local copies, waits for them, and re-layouts  2.49 us (6%)
    pallas_call x1, Pallas kernels, shards(): pl.pallas_call(kernel, out_shape=jax.ShapeDtypeStruct((out_toks, cols), b...  40.3 us
    unnamed x5, local copies, waits for them, and re-layouts  2.49 us

profile of v1, /device:TPU:1, one launch (start us, length us, event | category | flops | bytes accessed | tf_op | source)
XLA Modules:
  0.0 42.8 jit_solution(14198006088682070792)
XLA Ops:
  0.0 0.0 copy-start
  0.0 0.8 %copy-done = f32[512,16]{0,1:T(8,128)S(1)} copy-done((f32[512,16]{0,1:T(8,128)S(1)}, f32[512,16]{0,1:T(8,128)}, u32[]{:S(2)}) %copy-start) | copy-done | bytes 32792
  0.8 0.0 copy-start.1
  0.8 0.8 %copy-done.1 = f32[512,16]{0,1:T(8,128)S(1)} copy-done((f32[512,16]{0,1:T(8,128)S(1)}, f32[512,16]{0,1:T(8,128)}, u32[]{:S(2)}) %copy-start.1) | copy-done | bytes 32792
  1.5 40.3 %shard_map.55 = bf16[256,2048]{1,0:T(8,128)(2,1)S(1)} custom-call(bf16[512,1024]{1,0:T(8,128)(2,1)} %kv_hbm.1, bf16[512,1024]{1,0:T(8,128)(2,1)} %q_hbm.1, f32[16,512]{1,0:T(8,128)S(1)} %bitcast.2, f32[16,512]{1,0:T(8,128)S(1)} %bitcast.3, bf16[512,2048]{1,0:T(8,128)(2,1)} %w_hbm.1), custom_call_target="tpu_custom_call" | custom-call | flops 2147483648 | bytes 6291456 | tf_op jit(solution)/shard_map/pallas_call | solution.py:302
  41.8 1.0 %copy.7 = bf16[256,2048]{1,0:T(8,128)(2,1)} copy(bf16[256,2048]{1,0:T(8,128)(2,1)S(1)} %shard_map.55) | data formatting | bytes 2097152
Async XLA Ops:
  0.0 0.8 %copy-start = (f32[512,16]{0,1:T(8,128)S(1)}, f32[512,16]{0,1:T(8,128)}, u32[]{:S(2)}) copy-start(f32[512,16]{0,1:T(8,128)} %param.7) | copy-start | bytes 98308
  0.8 0.8 %copy-start.1 = (f32[512,16]{0,1:T(8,128)S(1)}, f32[512,16]{0,1:T(8,128)}, u32[]{:S(2)}) copy-start(f32[512,16]{0,1:T(8,128)} %param.8) | copy-start | bytes 98308

commit v2 on v1

--- a/solution.py
+++ b/solution.py
@@ -7,7 +7,9 @@
 
 NY, NZ, NX, NTP = 4, 4, 2, 4
 SUBS, LANES = 8, 128
-W_IMPORT = ("wrap", "direct", "wrap", "direct", "wrap", "direct", "wrap", "wrap")
+W_PIECES = (
+    ("near", 2), ("wrap", 3), ("near", 2), ("wrap", 3), ("near", 0), ("wrap", 1), ("wrap", 0), ("wrap", 1),
+)
 UNROLL = 16
 MESH = pl.DeviceIdType.MESH
 
@@ -106,7 +108,7 @@
 
     half = chans // 2
     parity = lax.rem(y + z, 2)
-    pieces = len(W_IMPORT)
+    pieces = len(W_PIECES)
     rows_in = half // pieces
 
     def rows_of(which, p):
@@ -117,18 +119,19 @@
     w_import, w_near, w_across = [], [], []
     for p in range(pieces):
         rows = rows_of(parity, p)
-        to = to_wrap if W_IMPORT[p] == "wrap" else to_tp[2]
+        to = to_wrap if W_PIECES[p][0] == "wrap" else to_tp[2]
+        onward = around[W_PIECES[p][1]]
         w_import.append(remote(w_hbm.at[rows], wf.at[2, rows], wi_send.at[p], wi_recv.at[p], to))
-        w_near.append(remote(wf.at[2, rows], wf.at[2, rows], wn_send.at[p], wn_recv.at[p], around[p % 4]))
+        w_near.append(remote(wf.at[2, rows], wf.at[2, rows], wn_send.at[p], wn_recv.at[p], onward))
         w_across.append(remote(wf.at[2, rows], wf.at[3, rows], wf_send.at[p], wf_recv.at[p], to_tp[1]))
     w_got = []
     for p in range(pieces):
         rows = rows_of(1 - parity, p)
-        w_got.append(remote(wf.at[2, rows], wf.at[2, rows], wn_send.at[p], wn_recv.at[p], around[p % 4]))
+        w_got.append(remote(wf.at[2, rows], wf.at[2, rows], wn_send.at[p], wn_recv.at[p], onward))
         w_across.append(
             remote(wf.at[2, rows], wf.at[3, rows], wf_send.at[pieces + p], wf_recv.at[pieces + p], to_tp[1])
         )
-    for copy in w_import:
+    for copy in w_import[:2]:
         copy.start()
     w_sib.start()
 
@@ -180,10 +183,11 @@
     block = float(toks)
     send_x = remote(s_own, s_x, x_sem.at[0], x_sem.at[1], to_x)
     send_x.start()
+    for copy in w_import[2:]:
+        copy.start()
     loads[3].wait()
     turn(q_v, qs, False)
     second_pass(0)
-    hand_on(0, 1)
     second_pass(1)
     send_x.wait_recv()
     dec = dec_t[...]
@@ -193,10 +197,10 @@
     sends_z = [remote(g_z.at[0], g_z.at[j], z_send.at[j], z_recv.at[j], to_z[j]) for j in range(1, NZ)]
     for send in sends_z:
         send.start()
+    hand_on(0, 1)
+    second_pass(2)
+    second_pass(3)
     hand_on(2, 3)
-    second_pass(2)
-    hand_on(4, 5)
-    second_pass(3)
     for send in sends_z:
         send.wait_recv()
     total = jnp.zeros_like(dec)
@@ -211,7 +215,6 @@
     sends_y = [remote(h_y.at[0], h_y.at[j], y_send.at[j], y_recv.at[j], to_y[j]) for j in range(1, NY)]
     for send in sends_y:
         send.start()
-    hand_on(6, 7)
     for send in sends_y:
         send.wait_recv()
     came = jnp.zeros_like(dec)
@@ -252,6 +255,7 @@
         gb[g] = (qs[g] * conv).astype(jnp.bfloat16)
         for send in (g_sends[g][1], g_sends[g][2], g_sends[g][0]):
             send.start()
+        hand_on(*((4, 5), (), (6,), (7,))[g])
 
     for p in range(pieces):
         w_got[p].wait_recv()
@@ -295,10 +299,11 @@
     cols = out_weight.shape[1]
     groups = chans // LANES
     out_toks = toks // NTP
-    pieces = len(W_IMPORT)
+    pieces = len(W_PIECES)
     bf16, f32 = jnp.bfloat16, jnp.float32
     small = (groups, modes, LANES)
     dma = pltpu.SemaphoreType.DMA
+    operands = (kv_product, query, decay_rate.T, residue.T, out_weight)
     return pl.pallas_call(
         kernel,
         out_shape=jax.ShapeDtypeStruct((out_toks, cols), bf16),
@@ -349,7 +354,7 @@
         cost_estimate=pl.CostEstimate(
             flops=2 * out_toks * cols * chans * NTP, bytes_accessed=6 * 1024 * 1024, transcendentals=0
         ),
-    )(kv_product, query, decay_rate.T, residue.T, out_weight)
+    )(*(pltpu.with_memory_space_constraint(a, pltpu.HBM) for a in operands))
 
 
 def solution(mesh):

time: 43 us -> 35.5 us (0.83)
  Pallas kernels: 40.3 us -> 34.4 us
  local copies, waits for them, and re-layouts: 2.49 us -> 0.97 us
    pallas_call x1, Pallas kernels: 40.3 us -> 34.4 us  [shards(): pl.pallas_call(kernel, out_shape=jax.ShapeDtypeStruct((out_toks, cols), b...]
    unnamed x5 -> x1, local copies, waits for them, and re-layouts: 2.49 us -> 0.97 us
where the time goes in v2:
time: 35.5 us; the launch traced here: 35.4 us
  Pallas kernels  34.4 us (97%)
  local copies, waits for them, and re-layouts  0.97 us (3%)
    pallas_call x1, Pallas kernels, shards(): pl.pallas_call(kernel, out_shape=jax.ShapeDtypeStruct((out_toks, cols), b...  34.4 us
    unnamed x1, local copies, waits for them, and re-layouts  0.97 us

profile of v2, /device:TPU:1, one launch (start us, length us, event | category | flops | bytes accessed | tf_op | source)
XLA Modules:
  0.0 35.4 jit_solution(14570609242490252757)
XLA Ops:
  0.0 34.4 %shard_map.55 = bf16[256,2048]{1,0:T(8,128)(2,1)S(1)} custom-call(bf16[512,1024]{1,0:T(8,128)(2,1)} %kv_hbm.1, bf16[512,1024]{1,0:T(8,128)(2,1)} %q_hbm.1, f32[16,512]{1,0:T(8,128)} %bitcast.2, f32[16,512]{1,0:T(8,128)} %bitcast.3, bf16[512,2048]{1,0:T(8,128)(2,1)} %w_hbm.1), custom_call_target="tpu_custom_call" | custom-call | flops 2147483648 | bytes 6291456 | tf_op jit(solution)/shard_map/pallas_call | solution.py:307
  34.4 1.0 %copy.7 = bf16[256,2048]{1,0:T(8,128)(2,1)} copy(bf16[256,2048]{1,0:T(8,128)(2,1)S(1)} %shard_map.55) | data formatting | bytes 2097152

commit v3 on v1

v3 whole, which is shorter than its diff:
```python
import jax
import jax.numpy as jnp
from jax import lax
from jax.experimental import pallas as pl
from jax.experimental.pallas import tpu as pltpu
from jax.sharding import PartitionSpec as P

NY, NZ, NX, NTP = 4, 4, 2, 4
SUBS, LANES = 8, 128
W_ROWS = (32, 48, 32, 16)
UNROLL = 16
MESH = pl.DeviceIdType.MESH


def one_minus_exp(z):
    series = jnp.ones_like(z)
    for n in range(10, 1, -1):
        series = 1.0 - (z * (1.0 / n)) * series
    return jnp.where(z < 0.5, z * series, 1.0 - jnp.exp(-z))


def shift_rows(value, by, row):
    return jnp.where(row >= by, pltpu.roll(value, by, 0), 0.0)


def tree_sum(terms):
    while len(terms) > 1:
        terms = [a + b for a, b in zip(terms[::2], terms[1::2])]
    return terms[0]


def at(t):
    return pl.ds(pl.multiple_of(t * SUBS, SUBS), SUBS)


def kernel(
    kv_hbm, q_hbm, dec_hbm, res_hbm, w_hbm, out_ref,
    kv_v, q_v, dec_v, res_v, kv_far, q_far, dec_far, res_far, wf,
    xs, qs, ys, yn, dec_t, lam_t, wgt_t, wc_t, ends, loc, pw,
    s_all, h_y, inc, t_rows, t_out, t_in,
    xd, qd, yd, ynd, dec_d, lam_d, wgt_d, wc_d, loc_d, pw_d,
    gb, gin, gd, acc,
    loc_sem, s_send, s_recv, y_send, y_recv, far_send, far_recv, t_send, t_recv,
    wsib_sem, wi_send, wi_recv, wn_send, wn_recv, wa_send, wa_recv, g_send, g_recv,
):
    chans, toks = kv_v.shape
    modes = dec_v.shape[0]
    groups = chans // LANES
    near_groups = groups // 2
    far_chans = chans // 2
    far_groups = groups - near_groups
    sub_len = toks // SUBS
    out_toks, cols = out_ref.shape
    far_len = out_toks // SUBS
    seq = float(toks * NY * NZ * NX)
    block = float(toks)
    f32, bf16 = jnp.float32, jnp.bfloat16

    ctx, tp = lax.axis_index("ctx"), lax.axis_index("tp")
    x_hi = lax.rem(ctx, NX)
    z = lax.rem(ctx // NX, NZ)
    y = ctx // (NX * NZ)
    x_lo, core = tp // 2, lax.rem(tp, 2)

    def ctx_of(yy, zz, xx):
        return (yy * NZ + zz) * NX + xx

    partner_tp = [tp, x_lo * 2 + (1 - core), (1 - x_lo) * 2 + core, (1 - x_lo) * 2 + (1 - core)]
    to_plane = [
        [{"ctx": ctx_of(y, lax.rem(z + j, NZ), xx), "tp": tp} for xx in (x_hi, 1 - x_hi)] for j in range(NZ)
    ]
    to_y = [{"ctx": ctx_of(lax.rem(y + j, NY), z, x_hi), "tp": tp} for j in range(NY)]
    to_tp = [{"ctx": ctx, "tp": t} for t in partner_tp]
    to_wrap = {"ctx": ctx_of(y, z, 1 - x_hi), "tp": partner_tp[2]}
    plane = [(j, k) for j in range(NZ) for k in range(NX) if j or k]

    loads = [
        pltpu.make_async_copy(kv_hbm, kv_v, loc_sem.at[0]),
        pltpu.make_async_copy(dec_hbm, dec_v, loc_sem.at[1]),
        pltpu.make_async_copy(res_hbm, res_v, loc_sem.at[2]),
        pltpu.make_async_copy(q_hbm, q_v, loc_sem.at[3]),
        pltpu.make_async_copy(w_hbm, wf.at[0], loc_sem.at[4]),
    ]
    for load in loads:
        load.start()

    barrier = pltpu.get_barrier_semaphore()
    partners = [to_plane[j][k] for j, k in plane] + to_y[1:] + to_tp[1:] + [to_wrap]
    for partner in partners:
        pl.semaphore_signal(barrier, inc=1, device_id=partner, device_id_type=MESH)

    def remote(src, dst, send, recv, to):
        return pltpu.make_async_remote_copy(
            src_ref=src, dst_ref=dst, send_sem=send, recv_sem=recv, device_id=to, device_id_type=MESH
        )

    far_rows, far_cols = pl.ds(far_chans, far_chans), pl.ds(near_groups * LANES, far_chans)
    far = []
    for r in range(1, NTP):
        there = pl.ds(pl.multiple_of(partner_tp[r] * out_toks, out_toks), out_toks)
        pairs = (
            (kv_hbm.at[far_rows, there], kv_far), (q_hbm.at[far_rows, there], q_far),
            (dec_hbm.at[:, far_cols], dec_far), (res_hbm.at[:, far_cols], res_far),
        )
        far.append(
            [
                remote(src, dst.at[r - 1], far_send.at[r - 1, i], far_recv.at[r - 1, i], to_tp[r])
                for i, (src, dst) in enumerate(pairs)
            ]
        )

    quarter = chans // 4
    mine = lax.rem(z + 2 * y, 4)

    def rows_of(which, i):
        return pl.ds(pl.multiple_of(which * quarter + sum(W_ROWS[:i]), 16), W_ROWS[i])

    w_sib = remote(w_hbm, wf.at[1], wsib_sem.at[0], wsib_sem.at[1], to_tp[1])
    w_import, w_on, w_got, w_across = [], [], [], []
    for i in range(len(W_ROWS)):
        rows = rows_of(mine, i)
        w_import.append(remote(w_hbm.at[rows], wf.at[2, rows], wi_send.at[i], wi_recv.at[i], to_wrap))
        ways = (to_plane[1][0], to_plane[NZ - 1][0], to_y[1] if i % 2 == 0 else to_y[NY - 1])
        w_on.append([])
        w_got.append([])
        w_across.append([remote(wf.at[2, rows], wf.at[3, rows], wa_send.at[3, i], wa_recv.at[3, i], to_tp[1])])
        for way, (to, theirs) in enumerate(zip(ways, (lax.rem(mine + 3, 4), lax.rem(mine + 1, 4), lax.rem(mine + 2, 4)))):
            rows = rows_of(mine, i)
            w_on[i].append(remote(wf.at[2, rows], wf.at[2, rows], wn_send.at[way, i], wn_recv.at[way, i], to))
            rows = rows_of(theirs, i)
            w_got[i].append(remote(wf.at[2, rows], wf.at[2, rows], wn_send.at[way, i], wn_recv.at[way, i], to))
            w_across[i].append(
                remote(wf.at[2, rows], wf.at[3, rows], wa_send.at[way, i], wa_recv.at[way, i], to_tp[1])
            )

    def hand_on(i):
        w_import[i].wait_recv()
        w_on[i][0].start()
        w_on[i][1].start()
        w_across[i][0].start()

    def hand_across(i, *ways):
        for way in ways:
            w_got[i][way].wait_recv()
            w_across[i][1 + way].start()

    def coefficients(dec, res, dec_to, lam_to, wgt_to, wc_to, *where):
        wgt = res * jnp.sqrt(one_minus_exp(2.0 * dec))
        dec_to[where] = dec
        lam_to[where] = jnp.exp(-dec)
        wgt_to[where] = wgt
        wc_to[where] = wgt * one_minus_exp(seq * dec)

    loads[1].wait()
    loads[2].wait()
    for g in range(groups):
        lanes = slice(g * LANES, (g + 1) * LANES)
        coefficients(dec_v[:, lanes], res_v[:, lanes], dec_t, lam_t, wgt_t, wc_t, g)

    loads[0].wait()
    for g in range(groups):
        for s in range(SUBS):
            turned = kv_v[g * LANES:(g + 1) * LANES, s * sub_len:(s + 1) * sub_len].T.astype(f32)
            xs[g, pl.ds(s, sub_len, stride=SUBS), :] = turned

    pl.semaphore_wait(barrier, len(partners))
    w_import[0].start()
    far[1][0].start()
    for copy in far[0]:
        copy.start()
    w_sib.start()

    row = lax.broadcasted_iota(jnp.int32, (SUBS, LANES), 0)
    row_f = row.astype(f32)

    def wide(ref, *where):
        *lead, m = where
        return jnp.broadcast_to(ref[(*lead, slice(m, m + 1), slice(None))], (SUBS, LANES))

    zeros = tuple(jnp.zeros((SUBS, LANES), f32) for _ in range(modes))

    def first_pass(g, carry):
        lam = [wide(lam_t, g, m) for m in range(modes)]

        def step(t, states):
            x = xs[g, at(t), :]
            return tuple(l * u + x for l, u in zip(lam, states))

        states = lax.fori_loop(0, sub_len, step, zeros, unroll=UNROLL)
        for m in range(modes):
            ends[g, m] = states[m]
            decayed = states[m] * jnp.exp(-wide(dec_t, g, m) * ((SUBS - 1 - row_f) * float(sub_len)))
            s_all[0, 0, g, m:m + 1, :] = jnp.sum(decayed, axis=0, keepdims=True)
        return carry

    lax.fori_loop(0, groups, first_pass, 0)

    sends_s = [
        remote(
            s_all.at[0, 0], s_all.at[j, k], s_send.at[j, k], s_recv.at[j, k], to_plane[j][k]
        )
        for j, k in plane
    ]
    for send in sends_s:
        send.start()
    for r in (1, 2):
        far[r][2].start()
        far[r][3].start()
    far[2][0].start()
    far[1][1].start()
    far[2][1].start()
    for copy in w_import[1:]:
        copy.start()

    def run_starts(states, decs, length):
        state = shift_rows(states * one_minus_exp(seq * decs), 1, row)
        for by in (1, 2, 4):
            state += jnp.exp(-float(by * length) * decs) * shift_rows(state, by, row)
        return state, jnp.exp(-(row_f * float(length)) * decs)

    def prepare(g, carry):
        for m in range(modes):
            loc[g, m], pw[g, m] = run_starts(ends[g, m], wide(dec_t, g, m), sub_len)
        return carry

    def second_pass(g):
        lam = [wide(lam_t, g, m) for m in range(modes)]
        gain = [wide(wc_t, g, m) for m in range(modes)]

        def step(t, states):
            x = xs[g, at(t), :]
            states = tuple(l * u + x for l, u in zip(lam, states))
            ys[g, at(t), :] = tree_sum([c * u for c, u in zip(gain, states)])
            return states

        lax.fori_loop(0, sub_len, step, zeros, unroll=UNROLL)

    own_toks = pl.ds(pl.multiple_of(tp * out_toks, out_toks), out_toks)

    def far_pass(r):
        if r:
            for i in (0, 2, 3):
                far[r - 1][i].wait_recv()
        halves = out_toks // LANES
        for g in range(far_groups):
            lanes = slice(g * LANES, (g + 1) * LANES)
            if r:
                dec, res = dec_far[r - 1, :, lanes], res_far[r - 1, :, lanes]
            else:
                own = slice(far_chans + g * LANES, far_chans + (g + 1) * LANES)
                dec, res = dec_v[:, own], res_v[:, own]
            coefficients(dec, res, dec_d, lam_d, wgt_d, wc_d, r, g)
            for h in range(halves):
                if r:
                    tile = kv_far[r - 1, lanes, h * LANES:(h + 1) * LANES]
                else:
                    tile = kv_v[own, pl.ds(pl.multiple_of(tp * out_toks + h * LANES, LANES), LANES)]
                turned = tile.T.astype(f32)
                for s in range(SUBS // halves):
                    xd[r, g, pl.ds(h * (SUBS // halves) + s, far_len, stride=SUBS), :] = (
                        turned[s * far_len:(s + 1) * far_len]
                    )

        def of_group(g, carry):
            lam = [wide(lam_d, r, g, m) for m in range(modes)]
            gain = [wide(wc_d, r, g, m) for m in range(modes)]

            def step(t, states):
                x = xd[r, g, at(t), :]
                states = tuple(l * u + x for l, u in zip(lam, states))
                yd[r, g, at(t), :] = tree_sum([c * u for c, u in zip(gain, states)])
                return states

            states = lax.fori_loop(0, far_len, step, zeros, unroll=UNROLL)
            for m in range(modes):
                loc_d[r, g, m], pw_d[r, g, m] = run_starts(states[m], wide(dec_d, r, g, m), far_len)
            return carry

        lax.fori_loop(0, far_groups, of_group, 0)

    def turn_query(r):
        for g in range(far_groups):
            for h in range(out_toks // LANES):
                if r:
                    tile = q_far[r - 1, g * LANES:(g + 1) * LANES, h * LANES:(h + 1) * LANES]
                else:
                    own = slice(far_chans + g * LANES, far_chans + (g + 1) * LANES)
                    tile = q_v[own, pl.ds(pl.multiple_of(tp * out_toks + h * LANES, LANES), LANES)]
                qd[r, g, h * LANES:(h + 1) * LANES, :] = tile.T.astype(f32)

    for g in range(near_groups):
        second_pass(g)
    hand_on(0)
    far_pass(0)
    lax.fori_loop(0, groups, prepare, 0)
    loads[3].wait()
    for g in range(near_groups):
        for s in range(SUBS):
            turned = q_v[g * LANES:(g + 1) * LANES, s * sub_len:(s + 1) * sub_len].T.astype(f32)
            qs[g, s * sub_len:(s + 1) * sub_len, :] = turned
    turn_query(0)

    dec = dec_t[...]
    lam1 = jnp.exp(-block * dec)
    once = one_minus_exp(seq * dec)
    for send in sends_s:
        send.wait_recv()
    total = jnp.zeros_like(dec)
    before = jnp.zeros_like(dec)
    for j in range(NZ):
        same, across = s_all[j, 0], s_all[j, 1]
        part = jnp.where(x_hi == 0, across + lam1 * same, same + lam1 * across)
        after = (NZ - 1 - lax.rem(z + NZ - j, NZ)).astype(f32) * (block * NX)
        total += jnp.exp(-after * dec) * part
        if j:
            before += jnp.where(z >= j, jnp.exp(-(block * NX * (j - 1)) * dec) * part, 0.0)
    h_y[0] = total
    sends_y = [remote(h_y.at[0], h_y.at[j], y_send.at[j], y_recv.at[j], to_y[j]) for j in range(1, NY)]
    for send in sends_y:
        send.start()

    w_on[0][2].start()
    far_pass(1)
    hand_on(1)
    w_on[1][2].start()
    far_pass(2)
    far_pass(3)
    hand_across(0, 0, 1)

    for send in sends_y:
        send.wait_recv()
    came = jnp.zeros_like(dec)
    for j in range(1, NY + 1):
        came += jnp.exp(-(block * NX * NZ * (j - 1)) * dec) * h_y[j % NY]
    came = jnp.exp(-(z.astype(f32) * (block * NX)) * dec) * came + once * before
    inc[...] = jnp.where(x_hi == 0, came, lam1 * came + once * s_all[0, 1])

    for g in range(far_groups):
        for m in range(modes):
            all_g = near_groups + g
            t_rows[g, m * SUBS:(m + 1) * SUBS, :] = loc[all_g, m] + pw[all_g, m] * wide(inc, all_g, m)
        for k in range(NTP):
            t_out[k, g] = t_rows[g, pl.ds(k * (SUBS // NTP), modes, stride=SUBS), :]
    t_sends = [
        remote(t_out.at[partner_tp[r]], t_in.at[r - 1], t_send.at[r - 1], t_recv.at[r - 1], to_tp[r])
        for r in range(1, NTP)
    ]
    for r in (2, 3, 1):
        t_sends[r - 1].start()

    g_sends = [
        [
            remote(
                gb.at[g, pl.ds(pl.multiple_of(partner_tp[r] * out_toks, out_toks), out_toks)],
                gin.at[r - 1, g], g_send.at[r - 1, g], g_recv.at[r - 1, g], to_tp[r],
            )
            for r in range(1, NTP)
        ]
        for g in range(near_groups)
    ]
    for g in range(near_groups):
        start = [wide(wgt_t, g, m) * (loc[g, m] + pw[g, m] * wide(inc, g, m)) for m in range(modes)]
        lam = [wide(lam_t, g, m) for m in range(modes)]

        def step(t, states):
            states = tuple(l * u for l, u in zip(lam, states))
            yn[g, pl.ds(t, SUBS, stride=sub_len), :] = ys[g, at(t), :] + tree_sum(list(states))
            return states

        lax.fori_loop(0, sub_len, step, tuple(start), unroll=UNROLL)
        gb[g] = (qs[g] * yn[g].astype(bf16).astype(f32)).astype(bf16)
        for r in (2, 3, 1):
            g_sends[g][r - 1].start()

    hand_on(2)
    w_on[2][2].start()
    hand_across(0, 2)
    hand_across(1, 0, 1)

    def far_correct(r):
        if r:
            t_sends[r - 1].wait_recv()
            far[r - 1][1].wait_recv()
            turn_query(r)

        def of_group(g, carry):
            came = (lambda m: wide(t_in, r - 1, g, m)) if r else (lambda m: wide(t_out, tp, g, m))
            start = [
                wide(wgt_d, r, g, m) * (loc_d[r, g, m] + pw_d[r, g, m] * came(m)) for m in range(modes)
            ]
            lam = [wide(lam_d, r, g, m) for m in range(modes)]

            def step(t, states):
                states = tuple(l * u for l, u in zip(lam, states))
                ynd[pl.ds(t, SUBS, stride=far_len), :] = yd[r, g, at(t), :] + tree_sum(list(states))
                return states

            lax.fori_loop(0, far_len, step, tuple(start), unroll=UNROLL)
            gd[r, g] = (qd[r, g] * ynd[...].astype(bf16).astype(f32)).astype(bf16)
            return carry

        lax.fori_loop(0, far_groups, of_group, 0)

    far_correct(0)
    far_correct(1)
    hand_on(3)
    w_on[3][2].start()
    far_correct(2)
    hand_across(1, 2)
    hand_across(2, 0, 1, 2)
    far_correct(3)

    loads[4].wait()
    w_sib.wait_recv()
    for g in range(near_groups):
        g_sends[g][0].wait_recv()
    lhs = jnp.concatenate(
        [gb[g, own_toks, :] for g in range(near_groups)] + [gd[0, g] for g in range(far_groups)]
        + [gin[0, g] for g in range(near_groups)] + [gd[1, g] for g in range(far_groups)], axis=1
    )
    acc[...] = jnp.dot(lhs, jnp.concatenate([wf[0], wf[1]], axis=0), preferred_element_type=f32)
    hand_across(3, 0, 1, 2)
    for per_piece in w_across:
        for copy in per_piece:
            copy.wait_recv()
    lhs = jnp.concatenate([gd[r, g] for r in (2, 3) for g in range(far_groups)], axis=1)
    rhs = jnp.concatenate([wf[r, far_chans:, :] for r in (2, 3)], axis=0)
    acc[...] += jnp.dot(lhs, rhs, preferred_element_type=f32)
    for g in range(near_groups):
        rows = slice(g * LANES, (g + 1) * LANES)
        g_sends[g][1].wait_recv()
        g_sends[g][2].wait_recv()
        lhs = jnp.concatenate([gin[1, g], gin[2, g]], axis=1)
        rhs = jnp.concatenate([wf[2, rows, :], wf[3, rows, :]], axis=0)
        part = acc[...] + jnp.dot(lhs, rhs, preferred_element_type=f32)
        if g == near_groups - 1:
            out_ref[...] = part.astype(bf16)
        else:
            acc[...] = part

    for copy in [w_sib] + sends_s + sends_y + t_sends + w_import:
        copy.wait_send()
    for family in (far, w_on, w_across, g_sends):
        for part in family:
            for copy in part:
                copy.wait_send()


def shards(kv_product, query, decay_rate, residue, out_weight):
    chans, toks = kv_product.shape
    modes = decay_rate.shape[1]
    cols = out_weight.shape[1]
    groups = chans // LANES
    near, far = groups // 2, groups - groups // 2
    out_toks = toks // NTP
    bf16, f32 = jnp.bfloat16, jnp.float32
    small = (groups, modes, LANES)
    runs = (groups, modes, SUBS, LANES)
    far_block = (NTP - 1, chans // 2, out_toks)
    far_coef = (NTP - 1, modes, chans // 2)
    pieces = len(W_ROWS)
    vmem, dma = pltpu.VMEM, pltpu.SemaphoreType.DMA
    operands = (kv_product, query, decay_rate.T, residue.T, out_weight)
    return pl.pallas_call(
        kernel,
        out_shape=jax.ShapeDtypeStruct((out_toks, cols), bf16),
        in_specs=[pl.BlockSpec(memory_space=pltpu.HBM)] * 5,
        out_specs=pl.BlockSpec(memory_space=pltpu.VMEM),
        scratch_shapes=[
            vmem((chans, toks), bf16), vmem((chans, toks), bf16), vmem((modes, chans), f32), vmem((modes, chans), f32),
            vmem(far_block, bf16), vmem(far_block, bf16), vmem(far_coef, f32), vmem(far_coef, f32),
            vmem((NTP, chans, cols), bf16),
            vmem((groups, toks, LANES), f32), vmem((near, toks, LANES), f32),
            vmem((near, toks, LANES), f32), vmem((near, toks, LANES), f32),
            vmem(small, f32), vmem(small, f32), vmem(small, f32), vmem(small, f32),
            vmem(runs, f32), vmem(runs, f32), vmem(runs, f32),
            vmem((NZ, NX) + small, f32), vmem((NY,) + small, f32), vmem(small, f32),
            vmem((far, modes * SUBS, LANES), f32),
            vmem((NTP, far, modes, LANES), f32), vmem((NTP - 1, far, modes, LANES), f32),
            vmem((NTP, far, out_toks, LANES), f32), vmem((NTP, far, out_toks, LANES), f32),
            vmem((NTP, far, out_toks, LANES), f32), vmem((out_toks, LANES), f32),
            vmem((NTP, far, modes, LANES), f32), vmem((NTP, far, modes, LANES), f32),
            vmem((NTP, far, modes, LANES), f32), vmem((NTP, far, modes, LANES), f32),
            vmem((NTP, far, modes, SUBS, LANES), f32), vmem((NTP, far, modes, SUBS, LANES), f32),
            vmem((near, toks, LANES), bf16), vmem((NTP - 1, near, out_toks, LANES), bf16),
            vmem((NTP, far, out_toks, LANES), bf16), vmem((out_toks, cols), f32),
            dma((5,)), dma((NZ, NX)), dma((NZ, NX)), dma((NY,)), dma((NY,)),
            dma((NTP - 1, 4)), dma((NTP - 1, 4)), dma((NTP - 1,)), dma((NTP - 1,)),
            dma((2,)), dma((pieces,)), dma((pieces,)), dma((3, pieces)), dma((3, pieces)),
            dma((4, pieces)), dma((4, pieces)), dma((NTP - 1, near)), dma((NTP - 1, near)),
        ],
        compiler_params=pltpu.CompilerParams(
            collective_id=0, has_side_effects=True, vmem_limit_bytes=50 * 1024 * 1024
        ),
        cost_estimate=pl.CostEstimate(
            flops=2 * out_toks * cols * chans * NTP, bytes_accessed=6 * 1024 * 1024, transcendentals=0
        ),
    )(*(pltpu.with_memory_space_constraint(a, pltpu.HBM) for a in operands))


def solution(mesh):
    in_specs = (P("tp", "ctx"), P("tp", "ctx"), P("tp", None), P("tp", None), P("tp", None))
    out_specs = P(("ctx", "tp"), None)
    return jax.shard_map(shards, mesh=mesh, in_specs=in_specs, out_specs=out_specs, check_vma=False)
```

time: 43 us -> 36.6 us (0.85)
  Pallas kernels: 40.3 us -> 35.5 us
  local copies, waits for them, and re-layouts: 2.49 us -> 0.97 us
    pallas_call x1, Pallas kernels: 40.3 us -> 35.5 us  [shards(): pl.pallas_call(kernel, out_shape=jax.ShapeDtypeStruct((out_toks, cols), b...]
    unnamed x5 -> x1, local copies, waits for them, and re-layouts: 2.49 us -> 0.97 us
where the time goes in v3:
time: 36.6 us; the launch traced here: 36.5 us
  Pallas kernels  35.5 us (97%)
  local copies, waits for them, and re-layouts  0.97 us (3%)
    pallas_call x1, Pallas kernels, shards(): pl.pallas_call(kernel, out_shape=jax.ShapeDtypeStruct((out_toks, cols), b...  35.5 us
    unnamed x1, local copies, waits for them, and re-layouts  0.97 us

profile of v3, /device:TPU:1, one launch (start us, length us, event | category | flops | bytes accessed | tf_op | source)
XLA Modules:
  0.0 36.5 jit_solution(1007144087125863518)
XLA Ops:
  0.0 35.5 %shard_map.55 = bf16[256,2048]{1,0:T(8,128)(2,1)S(1)} custom-call(bf16[512,1024]{1,0:T(8,128)(2,1)} %kv_hbm.1, bf16[512,1024]{1,0:T(8,128)(2,1)} %q_hbm.1, f32[16,512]{1,0:T(8,128)} %bitcast.2, f32[16,512]{1,0:T(8,128)} %bitcast.3, bf16[512,2048]{1,0:T(8,128)(2,1)} %w_hbm.1), custom_call_target="tpu_custom_call" | custom-call | flops 2147483648 | bytes 6291456 | tf_op jit(solution)/shard_map/pallas_call | solution.py:464
  35.6 1.0 %copy.7 = bf16[256,2048]{1,0:T(8,128)(2,1)} copy(bf16[256,2048]{1,0:T(8,128)(2,1)S(1)} %shard_map.55) | data formatting | bytes 2097152

commit v4 on v3

--- a/solution.py
+++ b/solution.py
@@ -7,7 +7,9 @@
 
 NY, NZ, NX, NTP = 4, 4, 2, 4
 SUBS, LANES = 8, 128
-W_ROWS = (32, 48, 32, 16)
+W_PIECES = 8
+W_UNITS_Y = ((0, 2), (2, 2), (4, 1), (5, 1), (6, 1), (7, 1))
+W_UNITS_CORE = ((0, 4), (4, 2), (6, 1), (7, 1))
 UNROLL = 16
 MESH = pl.DeviceIdType.MESH
 
@@ -36,11 +38,11 @@
 def kernel(
     kv_hbm, q_hbm, dec_hbm, res_hbm, w_hbm, out_ref,
     kv_v, q_v, dec_v, res_v, kv_far, q_far, dec_far, res_far, wf,
-    xs, qs, ys, yn, dec_t, lam_t, wgt_t, wc_t, ends, loc, pw,
-    s_all, h_y, inc, t_rows, t_out, t_in,
-    xd, qd, yd, ynd, dec_d, lam_d, wgt_d, wc_d, loc_d, pw_d,
+    xs, qs, ys, yn, dec_t, lam_t, wgt_t, wc_t, once_t, run_t, ends, loc, pw,
+    s_own, s_x, g_z, h_y, inc, t_rows, t_out, t_in,
+    xd, qd, yd, ynd, dec_d, lam_d, wgt_d, wc_d, once_d, run_d, loc_d, pw_d,
     gb, gin, gd, acc,
-    loc_sem, s_send, s_recv, y_send, y_recv, far_send, far_recv, t_send, t_recv,
+    loc_sem, x_sem, z_send, z_recv, y_send, y_recv, far_send, far_recv, t_send, t_recv,
     wsib_sem, wi_send, wi_recv, wn_send, wn_recv, wa_send, wa_recv, g_send, g_recv,
 ):
     chans, toks = kv_v.shape
@@ -66,13 +68,11 @@
         return (yy * NZ + zz) * NX + xx
 
     partner_tp = [tp, x_lo * 2 + (1 - core), (1 - x_lo) * 2 + core, (1 - x_lo) * 2 + (1 - core)]
-    to_plane = [
-        [{"ctx": ctx_of(y, lax.rem(z + j, NZ), xx), "tp": tp} for xx in (x_hi, 1 - x_hi)] for j in range(NZ)
-    ]
+    to_x = {"ctx": ctx_of(y, z, 1 - x_hi), "tp": tp}
+    to_z = [{"ctx": ctx_of(y, lax.rem(z + j, NZ), x_hi), "tp": tp} for j in range(NZ)]
     to_y = [{"ctx": ctx_of(lax.rem(y + j, NY), z, x_hi), "tp": tp} for j in range(NY)]
     to_tp = [{"ctx": ctx, "tp": t} for t in partner_tp]
     to_wrap = {"ctx": ctx_of(y, z, 1 - x_hi), "tp": partner_tp[2]}
-    plane = [(j, k) for j in range(NZ) for k in range(NX) if j or k]
 
     loads = [
         pltpu.make_async_copy(kv_hbm, kv_v, loc_sem.at[0]),
@@ -85,7 +85,7 @@
         load.start()
 
     barrier = pltpu.get_barrier_semaphore()
-    partners = [to_plane[j][k] for j, k in plane] + to_y[1:] + to_tp[1:] + [to_wrap]
+    partners = [to_x] + to_z[1:] + to_y[1:] + to_tp[1:] + [to_wrap]
     for partner in partners:
         pl.semaphore_signal(barrier, inc=1, device_id=partner, device_id_type=MESH)
 
@@ -98,64 +98,98 @@
     far = []
     for r in range(1, NTP):
         there = pl.ds(pl.multiple_of(partner_tp[r] * out_toks, out_toks), out_toks)
-        pairs = (
-            (kv_hbm.at[far_rows, there], kv_far), (q_hbm.at[far_rows, there], q_far),
-            (dec_hbm.at[:, far_cols], dec_far), (res_hbm.at[:, far_cols], res_far),
-        )
+        pairs = [
+            (kv_hbm.at[pl.ds(far_chans + g * LANES, LANES), there], kv_far.at[r - 1, pl.ds(g * LANES, LANES)])
+            for g in range(far_groups)
+        ] + [
+            (dec_hbm.at[:, far_cols], dec_far.at[r - 1]), (res_hbm.at[:, far_cols], res_far.at[r - 1]),
+            (q_hbm.at[far_rows, there], q_far.at[r - 1]),
+        ]
         far.append(
             [
-                remote(src, dst.at[r - 1], far_send.at[r - 1, i], far_recv.at[r - 1, i], to_tp[r])
+                remote(src, dst, far_send.at[r - 1, i], far_recv.at[r - 1, i], to_tp[r])
                 for i, (src, dst) in enumerate(pairs)
             ]
         )
+    f_dec, f_res, f_q = far_groups, far_groups + 1, far_groups + 2
+
+    for i, array in ((f_dec, dec_far), (f_res, res_far)):
+        far[2][i] = remote(array.at[1], array.at[2], far_send.at[2, i], far_recv.at[2, i], to_tp[1])
 
     quarter = chans // 4
+    piece = quarter // W_PIECES
     mine = lax.rem(z + 2 * y, 4)
-
-    def rows_of(which, i):
-        return pl.ds(pl.multiple_of(which * quarter + sum(W_ROWS[:i]), 16), W_ROWS[i])
+    theirs = (lax.rem(mine + 3, 4), lax.rem(mine + 1, 4), lax.rem(mine + 2, 4))
+
+    def rows_of(which, first, count):
+        return pl.ds(pl.multiple_of(which * quarter + first * piece, 16), count * piece)
+
+    def pass_on(way, which, first, count, to):
+        rows = rows_of(which, first, count)
+        return remote(wf.at[2, rows], wf.at[2, rows], wn_send.at[way, first], wn_recv.at[way, first], to)
 
     w_sib = remote(w_hbm, wf.at[1], wsib_sem.at[0], wsib_sem.at[1], to_tp[1])
-    w_import, w_on, w_got, w_across = [], [], [], []
-    for i in range(len(W_ROWS)):
-        rows = rows_of(mine, i)
+    w_import, w_on_z, w_got_z = [], [], []
+    for i in range(W_PIECES):
+        rows = rows_of(mine, i, 1)
         w_import.append(remote(w_hbm.at[rows], wf.at[2, rows], wi_send.at[i], wi_recv.at[i], to_wrap))
-        ways = (to_plane[1][0], to_plane[NZ - 1][0], to_y[1] if i % 2 == 0 else to_y[NY - 1])
-        w_on.append([])
-        w_got.append([])
-        w_across.append([remote(wf.at[2, rows], wf.at[3, rows], wa_send.at[3, i], wa_recv.at[3, i], to_tp[1])])
-        for way, (to, theirs) in enumerate(zip(ways, (lax.rem(mine + 3, 4), lax.rem(mine + 1, 4), lax.rem(mine + 2, 4)))):
-            rows = rows_of(mine, i)
-            w_on[i].append(remote(wf.at[2, rows], wf.at[2, rows], wn_send.at[way, i], wn_recv.at[way, i], to))
-            rows = rows_of(theirs, i)
-            w_got[i].append(remote(wf.at[2, rows], wf.at[2, rows], wn_send.at[way, i], wn_recv.at[way, i], to))
-            w_across[i].append(
-                remote(wf.at[2, rows], wf.at[3, rows], wa_send.at[way, i], wa_recv.at[way, i], to_tp[1])
+        ways = (to_z[1], to_z[NZ - 1])
+        w_on_z.append([pass_on(way, mine, i, 1, ways[way]) for way in (0, 1)])
+        w_got_z.append([pass_on(way, theirs[way], i, 1, ways[way]) for way in (0, 1)])
+    w_on_y, w_got_y = {}, {}
+    for u, (first, count) in enumerate(W_UNITS_Y):
+        to = to_y[1] if u % 2 == 0 else to_y[NY - 1]
+        w_on_y[first] = pass_on(2, mine, first, count, to)
+        w_got_y[first] = pass_on(2, theirs[2], first, count, to)
+    w_across = []
+    for u, (first, count) in enumerate(W_UNITS_CORE):
+        w_across.append([])
+        for way, which in enumerate(theirs + (mine,)):
+            rows = rows_of(which, first, count)
+            w_across[u].append(
+                remote(wf.at[2, rows], wf.at[3, rows], wa_send.at[way, u], wa_recv.at[way, u], to_tp[1])
             )
 
     def hand_on(i):
         w_import[i].wait_recv()
-        w_on[i][0].start()
-        w_on[i][1].start()
-        w_across[i][0].start()
-
-    def hand_across(i, *ways):
+        w_on_z[i][0].start()
+        w_on_z[i][1].start()
+        for u, (first, count) in enumerate(W_UNITS_CORE):
+            if i == first + count - 1:
+                w_across[u][3].start()
+
+    def hand_across(u, *ways):
+        first, count = W_UNITS_CORE[u]
         for way in ways:
-            w_got[i][way].wait_recv()
-            w_across[i][1 + way].start()
-
-    def coefficients(dec, res, dec_to, lam_to, wgt_to, wc_to, *where):
+            for i in range(first, first + count):
+                if way < 2:
+                    w_got_z[i][way].wait_recv()
+                elif i in w_got_y:
+                    w_got_y[i].wait_recv()
+            w_across[u][way].start()
+
+    def coefficients(dec, res, length, *where):
+        refs, where = where[0], where[1:]
+        dec_to, lam_to, wgt_to, wc_to, once_to, run_to = refs
         wgt = res * jnp.sqrt(one_minus_exp(2.0 * dec))
+        once = one_minus_exp(seq * dec)
+        run = jnp.exp(-float(length) * dec)
         dec_to[where] = dec
         lam_to[where] = jnp.exp(-dec)
         wgt_to[where] = wgt
-        wc_to[where] = wgt * one_minus_exp(seq * dec)
-
+        wc_to[where] = wgt * once
+        once_to[where] = once
+        for i in range(3):
+            run_to[(i, *where)] = run
+            run = run * run
+
+    near_coefs = (dec_t, lam_t, wgt_t, wc_t, once_t, run_t)
+    far_coefs = (dec_d, lam_d, wgt_d, wc_d, once_d, run_d)
     loads[1].wait()
     loads[2].wait()
     for g in range(groups):
         lanes = slice(g * LANES, (g + 1) * LANES)
-        coefficients(dec_v[:, lanes], res_v[:, lanes], dec_t, lam_t, wgt_t, wc_t, g)
+        coefficients(dec_v[:, lanes], res_v[:, lanes], sub_len, near_coefs, g)
 
     loads[0].wait()
     for g in range(groups):
@@ -163,64 +197,55 @@
             turned = kv_v[g * LANES:(g + 1) * LANES, s * sub_len:(s + 1) * sub_len].T.astype(f32)
             xs[g, pl.ds(s, sub_len, stride=SUBS), :] = turned
 
+    row = lax.broadcasted_iota(jnp.int32, (SUBS, LANES), 0)
+    row_f = row.astype(f32)
+
+    def wide(ref, *where):
+        *lead, m = where
+        return jnp.broadcast_to(ref[(*lead, slice(m, m + 1), slice(None))], (SUBS, LANES))
+
+    zeros = tuple(jnp.zeros((SUBS, LANES), f32) for _ in range(modes))
+
+    def first_pass(g, carry):
+        lam = [wide(lam_t, g, m) for m in range(modes)]
+
+        def step(t, states):
+            x = xs[g, at(t), :]
+            return tuple(l * u + x for l, u in zip(lam, states))
+
+        states = lax.fori_loop(0, sub_len, step, zeros, unroll=UNROLL)
+        for m in range(modes):
+            ends[g, m] = states[m]
+            decayed = states[m] * jnp.exp(-wide(dec_t, g, m) * ((SUBS - 1 - row_f) * float(sub_len)))
+            s_own[g, m:m + 1, :] = jnp.sum(decayed, axis=0, keepdims=True)
+        return carry
+
+    lax.fori_loop(0, groups // 2, first_pass, 0)
     pl.semaphore_wait(barrier, len(partners))
     w_import[0].start()
     far[1][0].start()
     for copy in far[0]:
         copy.start()
     w_sib.start()
-
-    row = lax.broadcasted_iota(jnp.int32, (SUBS, LANES), 0)
-    row_f = row.astype(f32)
-
-    def wide(ref, *where):
-        *lead, m = where
-        return jnp.broadcast_to(ref[(*lead, slice(m, m + 1), slice(None))], (SUBS, LANES))
-
-    zeros = tuple(jnp.zeros((SUBS, LANES), f32) for _ in range(modes))
-
-    def first_pass(g, carry):
-        lam = [wide(lam_t, g, m) for m in range(modes)]
-
-        def step(t, states):
-            x = xs[g, at(t), :]
-            return tuple(l * u + x for l, u in zip(lam, states))
-
-        states = lax.fori_loop(0, sub_len, step, zeros, unroll=UNROLL)
-        for m in range(modes):
-            ends[g, m] = states[m]
-            decayed = states[m] * jnp.exp(-wide(dec_t, g, m) * ((SUBS - 1 - row_f) * float(sub_len)))
-            s_all[0, 0, g, m:m + 1, :] = jnp.sum(decayed, axis=0, keepdims=True)
-        return carry
-
-    lax.fori_loop(0, groups, first_pass, 0)
-
-    sends_s = [
-        remote(
-            s_all.at[0, 0], s_all.at[j, k], s_send.at[j, k], s_recv.at[j, k], to_plane[j][k]
-        )
-        for j, k in plane
-    ]
-    for send in sends_s:
-        send.start()
-    for r in (1, 2):
-        far[r][2].start()
-        far[r][3].start()
-    far[2][0].start()
-    far[1][1].start()
-    far[2][1].start()
+    lax.fori_loop(groups // 2, groups, first_pass, 0)
+
+    send_x = remote(s_own, s_x, x_sem.at[0], x_sem.at[1], to_x)
+    send_x.start()
+    for copy in (far[1][1], far[1][f_dec], far[1][f_res], far[2][0], far[2][1], far[1][f_q], far[2][f_q]):
+        copy.start()
     for copy in w_import[1:]:
         copy.start()
 
-    def run_starts(states, decs, length):
-        state = shift_rows(states * one_minus_exp(seq * decs), 1, row)
-        for by in (1, 2, 4):
-            state += jnp.exp(-float(by * length) * decs) * shift_rows(state, by, row)
-        return state, jnp.exp(-(row_f * float(length)) * decs)
+    def run_starts(states, coefs, length, *where):
+        dec_of, _, _, _, once_of, run_of = coefs
+        state = shift_rows(states * wide(once_of, *where), 1, row)
+        for i, by in enumerate((1, 2, 4)):
+            state += wide(run_of, i, *where) * shift_rows(state, by, row)
+        return state, jnp.exp(wide(dec_of, *where) * (row_f * -float(length)))
 
     def prepare(g, carry):
         for m in range(modes):
-            loc[g, m], pw[g, m] = run_starts(ends[g, m], wide(dec_t, g, m), sub_len)
+            loc[g, m], pw[g, m] = run_starts(ends[g, m], near_coefs, sub_len, g, m)
         return carry
 
     def second_pass(g):
@@ -239,7 +264,7 @@
 
     def far_pass(r):
         if r:
-            for i in (0, 2, 3):
+            for i in (0, 1) if r == 2 else (0, 1, f_dec, f_res):
                 far[r - 1][i].wait_recv()
         halves = out_toks // LANES
         for g in range(far_groups):
@@ -249,7 +274,7 @@
             else:
                 own = slice(far_chans + g * LANES, far_chans + (g + 1) * LANES)
                 dec, res = dec_v[:, own], res_v[:, own]
-            coefficients(dec, res, dec_d, lam_d, wgt_d, wc_d, r, g)
+            coefficients(dec, res, far_len, far_coefs, r, g)
             for h in range(halves):
                 if r:
                     tile = kv_far[r - 1, lanes, h * LANES:(h + 1) * LANES]
@@ -273,7 +298,7 @@
 
             states = lax.fori_loop(0, far_len, step, zeros, unroll=UNROLL)
             for m in range(modes):
-                loc_d[r, g, m], pw_d[r, g, m] = run_starts(states[m], wide(dec_d, r, g, m), far_len)
+                loc_d[r, g, m], pw_d[r, g, m] = run_starts(states[m], far_coefs, far_len, r, g, m)
             return carry
 
         lax.fori_loop(0, far_groups, of_group, 0)
@@ -288,52 +313,72 @@
                     tile = q_v[own, pl.ds(pl.multiple_of(tp * out_toks + h * LANES, LANES), LANES)]
                 qd[r, g, h * LANES:(h + 1) * LANES, :] = tile.T.astype(f32)
 
-    for g in range(near_groups):
-        second_pass(g)
-    hand_on(0)
+    dec = dec_t[...]
+    lam1 = jnp.exp(-block * dec)
+    second_pass(0)
+    second_pass(1)
     far_pass(0)
     lax.fori_loop(0, groups, prepare, 0)
+    hand_on(0)
+    send_x.wait_recv()
+    same, across = s_own[...], s_x[...]
+    g_z[0] = jnp.where(x_hi == 0, across + lam1 * same, same + lam1 * across)
+    sends_z = [remote(g_z.at[0], g_z.at[j], z_send.at[j], z_recv.at[j], to_z[j]) for j in range(1, NZ)]
+    for send in sends_z:
+        send.start()
+
     loads[3].wait()
     for g in range(near_groups):
         for s in range(SUBS):
             turned = q_v[g * LANES:(g + 1) * LANES, s * sub_len:(s + 1) * sub_len].T.astype(f32)
             qs[g, s * sub_len:(s + 1) * sub_len, :] = turned
     turn_query(0)
-
-    dec = dec_t[...]
-    lam1 = jnp.exp(-block * dec)
-    once = one_minus_exp(seq * dec)
-    for send in sends_s:
+    hand_on(1)
+    far_pass(1)
+    far[1][f_dec].wait_recv()
+    far[1][f_res].wait_recv()
+    far[2][f_dec].start()
+    far[2][f_res].start()
+    hand_on(2)
+    far_pass(2)
+    after = [(NZ - 1 - lax.rem(z + NZ - j, NZ)).astype(f32) * (block * NX) for j in range(NZ)]
+    by_total = [jnp.exp(-a * dec) for a in after]
+    by_before = [None] + [
+        jnp.where(z >= j, jnp.exp(-(block * NX * (j - 1)) * dec), 0.0) for j in range(1, NZ)
+    ]
+    for send in sends_z:
         send.wait_recv()
-    total = jnp.zeros_like(dec)
+    total = by_total[0] * g_z[0]
     before = jnp.zeros_like(dec)
-    for j in range(NZ):
-        same, across = s_all[j, 0], s_all[j, 1]
-        part = jnp.where(x_hi == 0, across + lam1 * same, same + lam1 * across)
-        after = (NZ - 1 - lax.rem(z + NZ - j, NZ)).astype(f32) * (block * NX)
-        total += jnp.exp(-after * dec) * part
-        if j:
-            before += jnp.where(z >= j, jnp.exp(-(block * NX * (j - 1)) * dec) * part, 0.0)
+    for j in range(1, NZ):
+        part = g_z[j]
+        total += by_total[j] * part
+        before += by_before[j] * part
     h_y[0] = total
     sends_y = [remote(h_y.at[0], h_y.at[j], y_send.at[j], y_recv.at[j], to_y[j]) for j in range(1, NY)]
     for send in sends_y:
         send.start()
 
-    w_on[0][2].start()
-    far_pass(1)
-    hand_on(1)
-    w_on[1][2].start()
-    far_pass(2)
+    w_on_y[0].start()
+    hand_on(3)
+    w_on_y[2].start()
+    hand_on(4)
+    w_on_y[4].start()
     far_pass(3)
-    hand_across(0, 0, 1)
-
+    hand_on(5)
+    w_on_y[5].start()
+
+    start_z = z.astype(f32) * (block * NX)
+    by_y = [jnp.exp(-(block * NX * NZ * (j - 1) + start_z) * dec) for j in range(1, NY + 1)]
+    once = once_t[...]
+    before = once * before
+    beside = once * s_x[...]
     for send in sends_y:
         send.wait_recv()
-    came = jnp.zeros_like(dec)
+    came = before
     for j in range(1, NY + 1):
-        came += jnp.exp(-(block * NX * NZ * (j - 1)) * dec) * h_y[j % NY]
-    came = jnp.exp(-(z.astype(f32) * (block * NX)) * dec) * came + once * before
-    inc[...] = jnp.where(x_hi == 0, came, lam1 * came + once * s_all[0, 1])
+        came += by_y[j - 1] * h_y[j % NY]
+    inc[...] = jnp.where(x_hi == 0, came, lam1 * came + beside)
 
     for g in range(far_groups):
         for m in range(modes):
@@ -371,16 +416,13 @@
         gb[g] = (qs[g] * yn[g].astype(bf16).astype(f32)).astype(bf16)
         for r in (2, 3, 1):
             g_sends[g][r - 1].start()
-
-    hand_on(2)
-    w_on[2][2].start()
-    hand_across(0, 2)
-    hand_across(1, 0, 1)
+        hand_on(6 + g)
+        w_on_y[6 + g].start()
 
     def far_correct(r):
         if r:
             t_sends[r - 1].wait_recv()
-            far[r - 1][1].wait_recv()
+            far[r - 1][f_q].wait_recv()
             turn_query(r)
 
         def of_group(g, carry):
@@ -402,13 +444,13 @@
         lax.fori_loop(0, far_groups, of_group, 0)
 
     far_correct(0)
+    hand_across(0, 0, 1, 2)
     far_correct(1)
-    hand_on(3)
-    w_on[3][2].start()
+    hand_across(1, 0, 1)
     far_correct(2)
     hand_across(1, 2)
+    far_correct(3)
     hand_across(2, 0, 1, 2)
-    far_correct(3)
 
     loads[4].wait()
     w_sib.wait_recv()
@@ -438,9 +480,9 @@
         else:
             acc[...] = part
 
-    for copy in [w_sib] + sends_s + sends_y + t_sends + w_import:
+    for copy in [w_sib, send_x] + sends_z + sends_y + t_sends + w_import + list(w_on_y.values()):
         copy.wait_send()
-    for family in (far, w_on, w_across, g_sends):
+    for family in (far, w_on_z, w_across, g_sends):
         for part in family:
             for copy in part:
                 copy.wait_send()
@@ -458,7 +500,7 @@
     runs = (groups, modes, SUBS, LANES)
     far_block = (NTP - 1, chans // 2, out_toks)
     far_coef = (NTP - 1, modes, chans // 2)
-    pieces = len(W_ROWS)
+    pieces = W_PIECES
     vmem, dma = pltpu.VMEM, pltpu.SemaphoreType.DMA
     operands = (kv_product, query, decay_rate.T, residue.T, out_weight)
     return pl.pallas_call(
@@ -472,22 +514,24 @@
             vmem((NTP, chans, cols), bf16),
             vmem((groups, toks, LANES), f32), vmem((near, toks, LANES), f32),
             vmem((near, toks, LANES), f32), vmem((near, toks, LANES), f32),
-            vmem(small, f32), vmem(small, f32), vmem(small, f32), vmem(small, f32),
+            vmem(small, f32), vmem(small, f32), vmem(small, f32), vmem(small, f32), vmem(small, f32),
+            vmem((3,) + small, f32),
             vmem(runs, f32), vmem(runs, f32), vmem(runs, f32),
-            vmem((NZ, NX) + small, f32), vmem((NY,) + small, f32), vmem(small, f32),
+            vmem(small, f32), vmem(small, f32), vmem((NZ,) + small, f32), vmem((NY,) + small, f32), vmem(small, f32),
             vmem((far, modes * SUBS, LANES), f32),
             vmem((NTP, far, modes, LANES), f32), vmem((NTP - 1, far, modes, LANES), f32),
             vmem((NTP, far, out_toks, LANES), f32), vmem((NTP, far, out_toks, LANES), f32),
             vmem((NTP, far, out_toks, LANES), f32), vmem((out_toks, LANES), f32),
             vmem((NTP, far, modes, LANES), f32), vmem((NTP, far, modes, LANES), f32),
             vmem((NTP, far, modes, LANES), f32), vmem((NTP, far, modes, LANES), f32),
+            vmem((NTP, far, modes, LANES), f32), vmem((3, NTP, far, modes, LANES), f32),
             vmem((NTP, far, modes, SUBS, LANES), f32), vmem((NTP, far, modes, SUBS, LANES), f32),
             vmem((near, toks, LANES), bf16), vmem((NTP - 1, near, out_toks, LANES), bf16),
             vmem((NTP, far, out_toks, LANES), bf16), vmem((out_toks, cols), f32),
-            dma((5,)), dma((NZ, NX)), dma((NZ, NX)), dma((NY,)), dma((NY,)),
-            dma((NTP - 1, 4)), dma((NTP - 1, 4)), dma((NTP - 1,)), dma((NTP - 1,)),
+            dma((5,)), dma((2,)), dma((NZ,)), dma((NZ,)), dma((NY,)), dma((NY,)),
+            dma((NTP - 1, far + 3)), dma((NTP - 1, far + 3)), dma((NTP - 1,)), dma((NTP - 1,)),
             dma((2,)), dma((pieces,)), dma((pieces,)), dma((3, pieces)), dma((3, pieces)),
-            dma((4, pieces)), dma((4, pieces)), dma((NTP - 1, near)), dma((NTP - 1, near)),
+            dma((4, len(W_UNITS_CORE))), dma((4, len(W_UNITS_CORE))), dma((NTP - 1, near)), dma((NTP - 1, near)),
         ],
         compiler_params=pltpu.CompilerParams(
             collective_id=0, has_side_effects=True, vmem_limit_bytes=50 * 1024 * 1024

time: 36.6 us -> 34.1 us (0.932)
  Pallas kernels: 35.5 us -> 33.1 us
    pallas_call x1, Pallas kernels: 35.5 us -> 33.1 us  [shards(): pl.pallas_call(kernel, out_shape=jax.ShapeDtypeStruct((out_toks, cols), b...]
where the time goes in v4:
time: 34.1 us
  Pallas kernels  33.1 us (97%)
  local copies, waits for them, and re-layouts  0.97 us (3%)
    pallas_call x1, Pallas kernels, shards(): pl.pallas_call(kernel, out_shape=jax.ShapeDtypeStruct((out_toks, cols), b...  33.1 us
    unnamed x1, local copies, waits for them, and re-layouts  0.97 us

profile of v4, /device:TPU:1, one launch (start us, length us, event | category | flops | bytes accessed | tf_op | source)
XLA Modules:
  0.0 34.1 jit_solution(16072639998059902878)
XLA Ops:
  0.0 33.1 %shard_map.55 = bf16[256,2048]{1,0:T(8,128)(2,1)S(1)} custom-call(bf16[512,1024]{1,0:T(8,128)(2,1)} %kv_hbm.1, bf16[512,1024]{1,0:T(8,128)(2,1)} %q_hbm.1, f32[16,512]{1,0:T(8,128)} %bitcast.2, f32[16,512]{1,0:T(8,128)} %bitcast.3, bf16[512,2048]{1,0:T(8,128)(2,1)} %w_hbm.1), custom_call_target="tpu_custom_call" | custom-call | flops 2147483648 | bytes 6291456 | tf_op jit(solution)/shard_map/pallas_call | solution.py:506
  33.1 1.0 %copy.7 = bf16[256,2048]{1,0:T(8,128)(2,1)} copy(bf16[256,2048]{1,0:T(8,128)(2,1)S(1)} %shard_map.55) | data formatting | bytes 2097152

commit v5 on v4

--- a/solution.py
+++ b/solution.py
@@ -75,13 +75,16 @@
     to_wrap = {"ctx": ctx_of(y, z, 1 - x_hi), "tp": partner_tp[2]}
 
     loads = [
-        pltpu.make_async_copy(kv_hbm, kv_v, loc_sem.at[0]),
-        pltpu.make_async_copy(dec_hbm, dec_v, loc_sem.at[1]),
-        pltpu.make_async_copy(res_hbm, res_v, loc_sem.at[2]),
-        pltpu.make_async_copy(q_hbm, q_v, loc_sem.at[3]),
-        pltpu.make_async_copy(w_hbm, wf.at[0], loc_sem.at[4]),
+        pltpu.make_async_copy(dec_hbm, dec_v, loc_sem.at[0]),
+        pltpu.make_async_copy(res_hbm, res_v, loc_sem.at[1]),
+        pltpu.make_async_copy(q_hbm, q_v, loc_sem.at[2]),
+        pltpu.make_async_copy(w_hbm, wf.at[0], loc_sem.at[3]),
     ]
-    for load in loads:
+    kv_rows = [pl.ds(g * LANES, LANES) for g in range(groups)]
+    kv_loads = [
+        pltpu.make_async_copy(kv_hbm.at[rows], kv_v.at[rows], loc_sem.at[4 + g]) for g, rows in enumerate(kv_rows)
+    ]
+    for load in loads[:2] + kv_loads + loads[2:]:
         load.start()
 
     barrier = pltpu.get_barrier_semaphore()
@@ -185,14 +188,14 @@
 
     near_coefs = (dec_t, lam_t, wgt_t, wc_t, once_t, run_t)
     far_coefs = (dec_d, lam_d, wgt_d, wc_d, once_d, run_d)
+    loads[0].wait()
     loads[1].wait()
-    loads[2].wait()
     for g in range(groups):
         lanes = slice(g * LANES, (g + 1) * LANES)
         coefficients(dec_v[:, lanes], res_v[:, lanes], sub_len, near_coefs, g)
 
-    loads[0].wait()
-    for g in range(groups):
+    def turn_near(g):
+        kv_loads[g].wait()
         for s in range(SUBS):
             turned = kv_v[g * LANES:(g + 1) * LANES, s * sub_len:(s + 1) * sub_len].T.astype(f32)
             xs[g, pl.ds(s, sub_len, stride=SUBS), :] = turned
@@ -206,7 +209,7 @@
 
     zeros = tuple(jnp.zeros((SUBS, LANES), f32) for _ in range(modes))
 
-    def first_pass(g, carry):
+    def first_pass(g):
         lam = [wide(lam_t, g, m) for m in range(modes)]
 
         def step(t, states):
@@ -218,16 +221,19 @@
             ends[g, m] = states[m]
             decayed = states[m] * jnp.exp(-wide(dec_t, g, m) * ((SUBS - 1 - row_f) * float(sub_len)))
             s_own[g, m:m + 1, :] = jnp.sum(decayed, axis=0, keepdims=True)
-        return carry
-
-    lax.fori_loop(0, groups // 2, first_pass, 0)
+
+    for g in range(groups // 2):
+        turn_near(g)
+        first_pass(g)
     pl.semaphore_wait(barrier, len(partners))
     w_import[0].start()
     far[1][0].start()
     for copy in far[0]:
         copy.start()
     w_sib.start()
-    lax.fori_loop(groups // 2, groups, first_pass, 0)
+    for g in range(groups // 2, groups):
+        turn_near(g)
+        first_pass(g)
 
     send_x = remote(s_own, s_x, x_sem.at[0], x_sem.at[1], to_x)
     send_x.start()
@@ -243,9 +249,11 @@
             state += wide(run_of, i, *where) * shift_rows(state, by, row)
         return state, jnp.exp(wide(dec_of, *where) * (row_f * -float(length)))
 
-    def prepare(g, carry):
+    def prepare(g, carry, weighted):
         for m in range(modes):
-            loc[g, m], pw[g, m] = run_starts(ends[g, m], near_coefs, sub_len, g, m)
+            state, decay = run_starts(ends[g, m], near_coefs, sub_len, g, m)
+            wgt = wide(wgt_t, g, m) if weighted else 1.0
+            loc[g, m], pw[g, m] = wgt * state, wgt * decay
         return carry
 
     def second_pass(g):
@@ -298,7 +306,9 @@
 
             states = lax.fori_loop(0, far_len, step, zeros, unroll=UNROLL)
             for m in range(modes):
-                loc_d[r, g, m], pw_d[r, g, m] = run_starts(states[m], far_coefs, far_len, r, g, m)
+                state, decay = run_starts(states[m], far_coefs, far_len, r, g, m)
+                wgt = wide(wgt_d, r, g, m)
+                loc_d[r, g, m], pw_d[r, g, m] = wgt * state, wgt * decay
             return carry
 
         lax.fori_loop(0, far_groups, of_group, 0)
@@ -318,8 +328,8 @@
     second_pass(0)
     second_pass(1)
     far_pass(0)
-    lax.fori_loop(0, groups, prepare, 0)
-    hand_on(0)
+    lax.fori_loop(0, near_groups, lambda g, carry: prepare(g, carry, True), 0)
+    lax.fori_loop(near_groups, groups, lambda g, carry: prepare(g, carry, False), 0)
     send_x.wait_recv()
     same, across = s_own[...], s_x[...]
     g_z[0] = jnp.where(x_hi == 0, across + lam1 * same, same + lam1 * across)
@@ -327,20 +337,21 @@
     for send in sends_z:
         send.start()
 
-    loads[3].wait()
+    loads[2].wait()
     for g in range(near_groups):
         for s in range(SUBS):
             turned = q_v[g * LANES:(g + 1) * LANES, s * sub_len:(s + 1) * sub_len].T.astype(f32)
             qs[g, s * sub_len:(s + 1) * sub_len, :] = turned
     turn_query(0)
-    hand_on(1)
+    hand_on(0)
     far_pass(1)
     far[1][f_dec].wait_recv()
     far[1][f_res].wait_recv()
     far[2][f_dec].start()
     far[2][f_res].start()
+    hand_on(1)
+    far_pass(2)
     hand_on(2)
-    far_pass(2)
     after = [(NZ - 1 - lax.rem(z + NZ - j, NZ)).astype(f32) * (block * NX) for j in range(NZ)]
     by_total = [jnp.exp(-a * dec) for a in after]
     by_before = [None] + [
@@ -360,13 +371,11 @@
         send.start()
 
     w_on_y[0].start()
+    far_pass(3)
     hand_on(3)
     w_on_y[2].start()
     hand_on(4)
     w_on_y[4].start()
-    far_pass(3)
-    hand_on(5)
-    w_on_y[5].start()
 
     start_z = z.astype(f32) * (block * NX)
     by_y = [jnp.exp(-(block * NX * NZ * (j - 1) + start_z) * dec) for j in range(1, NY + 1)]
@@ -392,6 +401,9 @@
     ]
     for r in (2, 3, 1):
         t_sends[r - 1].start()
+    for i in (5, 6):
+        hand_on(i)
+        w_on_y[i].start()
 
     g_sends = [
         [
@@ -404,7 +416,7 @@
         for g in range(near_groups)
     ]
     for g in range(near_groups):
-        start = [wide(wgt_t, g, m) * (loc[g, m] + pw[g, m] * wide(inc, g, m)) for m in range(modes)]
+        start = [loc[g, m] + pw[g, m] * wide(inc, g, m) for m in range(modes)]
         lam = [wide(lam_t, g, m) for m in range(modes)]
 
         def step(t, states):
@@ -416,8 +428,9 @@
         gb[g] = (qs[g] * yn[g].astype(bf16).astype(f32)).astype(bf16)
         for r in (2, 3, 1):
             g_sends[g][r - 1].start()
-        hand_on(6 + g)
-        w_on_y[6 + g].start()
+        if g == 0:
+            hand_on(7)
+            w_on_y[7].start()
 
     def far_correct(r):
         if r:
@@ -427,9 +440,7 @@
 
         def of_group(g, carry):
             came = (lambda m: wide(t_in, r - 1, g, m)) if r else (lambda m: wide(t_out, tp, g, m))
-            start = [
-                wide(wgt_d, r, g, m) * (loc_d[r, g, m] + pw_d[r, g, m] * came(m)) for m in range(modes)
-            ]
+            start = [loc_d[r, g, m] + pw_d[r, g, m] * came(m) for m in range(modes)]
             lam = [wide(lam_d, r, g, m) for m in range(modes)]
 
             def step(t, states):
@@ -449,10 +460,12 @@
     hand_across(1, 0, 1)
     far_correct(2)
     hand_across(1, 2)
+    hand_across(2, 0, 1)
     far_correct(3)
-    hand_across(2, 0, 1, 2)
-
-    loads[4].wait()
+    hand_across(2, 2)
+    hand_across(3, 0, 1, 2)
+
+    loads[3].wait()
     w_sib.wait_recv()
     for g in range(near_groups):
         g_sends[g][0].wait_recv()
@@ -461,7 +474,6 @@
         + [gin[0, g] for g in range(near_groups)] + [gd[1, g] for g in range(far_groups)], axis=1
     )
     acc[...] = jnp.dot(lhs, jnp.concatenate([wf[0], wf[1]], axis=0), preferred_element_type=f32)
-    hand_across(3, 0, 1, 2)
     for per_piece in w_across:
         for copy in per_piece:
             copy.wait_recv()
@@ -528,7 +540,7 @@
             vmem((NTP, far, modes, SUBS, LANES), f32), vmem((NTP, far, modes, SUBS, LANES), f32),
             vmem((near, toks, LANES), bf16), vmem((NTP - 1, near, out_toks, LANES), bf16),
             vmem((NTP, far, out_toks, LANES), bf16), vmem((out_toks, cols), f32),
-            dma((5,)), dma((2,)), dma((NZ,)), dma((NZ,)), dma((NY,)), dma((NY,)),
+            dma((4 + groups,)), dma((2,)), dma((NZ,)), dma((NZ,)), dma((NY,)), dma((NY,)),
             dma((NTP - 1, far + 3)), dma((NTP - 1, far + 3)), dma((NTP - 1,)), dma((NTP - 1,)),
             dma((2,)), dma((pieces,)), dma((pieces,)), dma((3, pieces)), dma((3, pieces)),
             dma((4, len(W_UNITS_CORE))), dma((4, len(W_UNITS_CORE))), dma((NTP - 1, near)), dma((NTP - 1, near)),

time: 34.1 us -> 32.8 us (0.962)
  Pallas kernels: 33.1 us -> 31.7 us
    pallas_call x1, Pallas kernels: 33.1 us -> 31.7 us  [shards(): pl.pallas_call(kernel, out_shape=jax.ShapeDtypeStruct((out_toks, cols), b...]
where the time goes in v5:
time: 32.8 us; the launch traced here: 32.7 us
  Pallas kernels  31.7 us (97%)
  local copies, waits for them, and re-layouts  0.97 us (3%)
    pallas_call x1, Pallas kernels, shards(): pl.pallas_call(kernel, out_shape=jax.ShapeDtypeStruct((out_toks, cols), b...  31.7 us
    unnamed x1, local copies, waits for them, and re-layouts  0.97 us

profile of v5, /device:TPU:1, one launch (start us, length us, event | category | flops | bytes accessed | tf_op | source)
XLA Modules:
  0.0 32.7 jit_solution(3969977398045857357)
XLA Ops:
  0.0 31.7 %shard_map.55 = bf16[256,2048]{1,0:T(8,128)(2,1)S(1)} custom-call(bf16[512,1024]{1,0:T(8,128)(2,1)} %kv_hbm.1, bf16[512,1024]{1,0:T(8,128)(2,1)} %q_hbm.1, f32[16,512]{1,0:T(8,128)} %bitcast.2, f32[16,512]{1,0:T(8,128)} %bitcast.3, bf16[512,2048]{1,0:T(8,128)(2,1)} %w_hbm.1), custom_call_target="tpu_custom_call" | custom-call | flops 2147483648 | bytes 6291456 | tf_op jit(solution)/shard_map/pallas_call | solution.py:518
  31.7 1.0 %copy.7 = bf16[256,2048]{1,0:T(8,128)(2,1)} copy(bf16[256,2048]{1,0:T(8,128)(2,1)S(1)} %shard_map.55) | data formatting | bytes 2097152

commit v6 on v5

--- a/solution.py
+++ b/solution.py
@@ -8,8 +8,8 @@
 NY, NZ, NX, NTP = 4, 4, 2, 4
 SUBS, LANES = 8, 128
 W_PIECES = 8
-W_UNITS_Y = ((0, 2), (2, 2), (4, 1), (5, 1), (6, 1), (7, 1))
-W_UNITS_CORE = ((0, 4), (4, 2), (6, 1), (7, 1))
+W_ORDER = (0, 4, 1, 5, 2, 6, 3, 7)
+W_UNITS = ((0, 2), (2, 1), (3, 1), (4, 2), (6, 1), (7, 1))
 UNROLL = 16
 MESH = pl.DeviceIdType.MESH
 
@@ -121,54 +121,53 @@
 
     quarter = chans // 4
     piece = quarter // W_PIECES
-    mine = lax.rem(z + 2 * y, 4)
-    theirs = (lax.rem(mine + 3, 4), lax.rem(mine + 1, 4), lax.rem(mine + 2, 4))
 
     def rows_of(which, first, count):
         return pl.ds(pl.multiple_of(which * quarter + first * piece, 16), count * piece)
 
-    def pass_on(way, which, first, count, to):
-        rows = rows_of(which, first, count)
-        return remote(wf.at[2, rows], wf.at[2, rows], wn_send.at[way, first], wn_recv.at[way, first], to)
-
     w_sib = remote(w_hbm, wf.at[1], wsib_sem.at[0], wsib_sem.at[1], to_tp[1])
-    w_import, w_on_z, w_got_z = [], [], []
+    holds = []
+    for mine in (lax.rem(z + 2 * y, 4), lax.rem(y + 2 * z, 4)):
+        holds.append((lax.rem(mine + 3, 4), lax.rem(mine + 1, 4), lax.rem(mine + 2, 4), mine))
+    w_import, w_on, w_got = [], [], []
     for i in range(W_PIECES):
-        rows = rows_of(mine, i, 1)
-        w_import.append(remote(w_hbm.at[rows], wf.at[2, rows], wi_send.at[i], wi_recv.at[i], to_wrap))
-        ways = (to_z[1], to_z[NZ - 1])
-        w_on_z.append([pass_on(way, mine, i, 1, ways[way]) for way in (0, 1)])
-        w_got_z.append([pass_on(way, theirs[way], i, 1, ways[way]) for way in (0, 1)])
-    w_on_y, w_got_y = {}, {}
-    for u, (first, count) in enumerate(W_UNITS_Y):
-        to = to_y[1] if u % 2 == 0 else to_y[NY - 1]
-        w_on_y[first] = pass_on(2, mine, first, count, to)
-        w_got_y[first] = pass_on(2, theirs[2], first, count, to)
+        by_y = i // (W_PIECES // 2)
+        turn_to, half_to = ((to_z, to_y), (to_y, to_z))[by_y]
+        ways = (turn_to[1], turn_to[NZ - 1], half_to[1 if i % 2 == 0 else NY - 1])
+        mine = rows_of(holds[by_y][3], i, 1)
+        w_import.append(remote(w_hbm.at[mine], wf.at[2, mine], wi_send.at[i], wi_recv.at[i], to_wrap))
+        w_on.append([])
+        w_got.append([])
+        for way, to in enumerate(ways):
+            theirs = rows_of(holds[by_y][way], i, 1)
+            w_on[i].append(remote(wf.at[2, mine], wf.at[2, mine], wn_send.at[way, i], wn_recv.at[way, i], to))
+            w_got[i].append(remote(wf.at[2, theirs], wf.at[2, theirs], wn_send.at[way, i], wn_recv.at[way, i], to))
     w_across = []
-    for u, (first, count) in enumerate(W_UNITS_CORE):
+    for u, (first, count) in enumerate(W_UNITS):
         w_across.append([])
-        for way, which in enumerate(theirs + (mine,)):
+        for way, which in enumerate(holds[first // (W_PIECES // 2)]):
             rows = rows_of(which, first, count)
             w_across[u].append(
                 remote(wf.at[2, rows], wf.at[3, rows], wa_send.at[way, u], wa_recv.at[way, u], to_tp[1])
             )
 
+    def on_by_y(i):
+        for way in ((2,), (0, 1))[i // (W_PIECES // 2)]:
+            w_on[i][way].start()
+
     def hand_on(i):
         w_import[i].wait_recv()
-        w_on_z[i][0].start()
-        w_on_z[i][1].start()
-        for u, (first, count) in enumerate(W_UNITS_CORE):
+        for way in ((0, 1), (2,))[i // (W_PIECES // 2)]:
+            w_on[i][way].start()
+        for u, (first, count) in enumerate(W_UNITS):
             if i == first + count - 1:
                 w_across[u][3].start()
 
-    def hand_across(u, *ways):
-        first, count = W_UNITS_CORE[u]
-        for way in ways:
+    def hand_across(u):
+        first, count = W_UNITS[u]
+        for way in range(3):
             for i in range(first, first + count):
-                if way < 2:
-                    w_got_z[i][way].wait_recv()
-                elif i in w_got_y:
-                    w_got_y[i].wait_recv()
+                w_got[i][way].wait_recv()
             w_across[u][way].start()
 
     def coefficients(dec, res, length, *where):
@@ -226,7 +225,7 @@
         turn_near(g)
         first_pass(g)
     pl.semaphore_wait(barrier, len(partners))
-    w_import[0].start()
+    w_import[W_ORDER[0]].start()
     far[1][0].start()
     for copy in far[0]:
         copy.start()
@@ -237,9 +236,9 @@
 
     send_x = remote(s_own, s_x, x_sem.at[0], x_sem.at[1], to_x)
     send_x.start()
-    for copy in (far[1][1], far[1][f_dec], far[1][f_res], far[2][0], far[2][1], far[1][f_q], far[2][f_q]):
-        copy.start()
-    for copy in w_import[1:]:
+    rest = (far[1][1], far[1][f_dec], far[1][f_res], far[2][0], far[2][1], far[1][f_q], far[2][f_q])
+    for i, copy in zip(W_ORDER[1:], rest):
+        w_import[i].start()
         copy.start()
 
     def run_starts(states, coefs, length, *where):
@@ -343,15 +342,17 @@
             turned = q_v[g * LANES:(g + 1) * LANES, s * sub_len:(s + 1) * sub_len].T.astype(f32)
             qs[g, s * sub_len:(s + 1) * sub_len, :] = turned
     turn_query(0)
-    hand_on(0)
+    hand_on(W_ORDER[0])
+    on_by_y(W_ORDER[0])
     far_pass(1)
     far[1][f_dec].wait_recv()
     far[1][f_res].wait_recv()
     far[2][f_dec].start()
     far[2][f_res].start()
-    hand_on(1)
+    hand_on(W_ORDER[1])
+    on_by_y(W_ORDER[1])
     far_pass(2)
-    hand_on(2)
+    hand_on(W_ORDER[2])
     after = [(NZ - 1 - lax.rem(z + NZ - j, NZ)).astype(f32) * (block * NX) for j in range(NZ)]
     by_total = [jnp.exp(-a * dec) for a in after]
     by_before = [None] + [
@@ -370,12 +371,11 @@
     for send in sends_y:
         send.start()
 
-    w_on_y[0].start()
+    on_by_y(W_ORDER[2])
     far_pass(3)
-    hand_on(3)
-    w_on_y[2].start()
-    hand_on(4)
-    w_on_y[4].start()
+    for i in W_ORDER[3:5]:
+        hand_on(i)
+        on_by_y(i)
 
     start_z = z.astype(f32) * (block * NX)
     by_y = [jnp.exp(-(block * NX * NZ * (j - 1) + start_z) * dec) for j in range(1, NY + 1)]
@@ -401,9 +401,9 @@
     ]
     for r in (2, 3, 1):
         t_sends[r - 1].start()
-    for i in (5, 6):
+    for i in W_ORDER[5:7]:
         hand_on(i)
-        w_on_y[i].start()
+        on_by_y(i)
 
     g_sends = [
         [
@@ -429,8 +429,8 @@
         for r in (2, 3, 1):
             g_sends[g][r - 1].start()
         if g == 0:
-            hand_on(7)
-            w_on_y[7].start()
+            hand_on(W_ORDER[7])
+            on_by_y(W_ORDER[7])
 
     def far_correct(r):
         if r:
@@ -455,15 +455,15 @@
         lax.fori_loop(0, far_groups, of_group, 0)
 
     far_correct(0)
-    hand_across(0, 0, 1, 2)
+    hand_across(0)
     far_correct(1)
-    hand_across(1, 0, 1)
+    hand_across(3)
     far_correct(2)
-    hand_across(1, 2)
-    hand_across(2, 0, 1)
+    hand_across(1)
+    hand_across(4)
     far_correct(3)
-    hand_across(2, 2)
-    hand_across(3, 0, 1, 2)
+    hand_across(2)
+    hand_across(5)
 
     loads[3].wait()
     w_sib.wait_recv()
@@ -492,9 +492,9 @@
         else:
             acc[...] = part
 
-    for copy in [w_sib, send_x] + sends_z + sends_y + t_sends + w_import + list(w_on_y.values()):
+    for copy in [w_sib, send_x] + sends_z + sends_y + t_sends + w_import:
         copy.wait_send()
-    for family in (far, w_on_z, w_across, g_sends):
+    for family in (far, w_on, w_across, g_sends):
         for part in family:
             for copy in part:
                 copy.wait_send()
@@ -543,7 +543,7 @@
             dma((4 + groups,)), dma((2,)), dma((NZ,)), dma((NZ,)), dma((NY,)), dma((NY,)),
             dma((NTP - 1, far + 3)), dma((NTP - 1, far + 3)), dma((NTP - 1,)), dma((NTP - 1,)),
             dma((2,)), dma((pieces,)), dma((pieces,)), dma((3, pieces)), dma((3, pieces)),
-            dma((4, len(W_UNITS_CORE))), dma((4, len(W_UNITS_CORE))), dma((NTP - 1, near)), dma((NTP - 1, near)),
+            dma((4, len(W_UNITS))), dma((4, len(W_UNITS))), dma((NTP - 1, near)), dma((NTP - 1, near)),
         ],
         compiler_params=pltpu.CompilerParams(
             collective_id=0, has_side_effects=True, vmem_limit_bytes=50 * 1024 * 1024

time: 32.8 us -> 32.7 us (level)
  no operation moved by 1% of the time
where the time goes in v6:
time: 32.7 us; the launch traced here: 32.6 us
  Pallas kernels  31.6 us (97%)
  local copies, waits for them, and re-layouts  0.97 us (3%)
    pallas_call x1, Pallas kernels, shards(): pl.pallas_call(kernel, out_shape=jax.ShapeDtypeStruct((out_toks, cols), b...  31.6 us
    unnamed x1, local copies, waits for them, and re-layouts  0.97 us

profile of v6, /device:TPU:1, one launch (start us, length us, event | category | flops | bytes accessed | tf_op | source)
XLA Modules:
  0.0 32.6 jit_solution(2288538149389237657)
XLA Ops:
  0.0 31.6 %shard_map.55 = bf16[256,2048]{1,0:T(8,128)(2,1)S(1)} custom-call(bf16[512,1024]{1,0:T(8,128)(2,1)} %kv_hbm.1, bf16[512,1024]{1,0:T(8,128)(2,1)} %q_hbm.1, f32[16,512]{1,0:T(8,128)} %bitcast.2, f32[16,512]{1,0:T(8,128)} %bitcast.3, bf16[512,2048]{1,0:T(8,128)(2,1)} %w_hbm.1), custom_call_target="tpu_custom_call" | custom-call | flops 2147483648 | bytes 6291456 | tf_op jit(solution)/shard_map/pallas_call | solution.py:518
  31.6 1.0 %copy.7 = bf16[256,2048]{1,0:T(8,128)(2,1)} copy(bf16[256,2048]{1,0:T(8,128)(2,1)S(1)} %shard_map.55) | data formatting | bytes 2097152

commit v7 on v6

--- a/solution.py
+++ b/solution.py
@@ -10,7 +10,7 @@
 W_PIECES = 8
 W_ORDER = (0, 4, 1, 5, 2, 6, 3, 7)
 W_UNITS = ((0, 2), (2, 1), (3, 1), (4, 2), (6, 1), (7, 1))
-UNROLL = 16
+UNROLL = 32
 MESH = pl.DeviceIdType.MESH
 
 
@@ -352,7 +352,6 @@
     hand_on(W_ORDER[1])
     on_by_y(W_ORDER[1])
     far_pass(2)
-    hand_on(W_ORDER[2])
     after = [(NZ - 1 - lax.rem(z + NZ - j, NZ)).astype(f32) * (block * NX) for j in range(NZ)]
     by_total = [jnp.exp(-a * dec) for a in after]
     by_before = [None] + [
@@ -371,6 +370,7 @@
     for send in sends_y:
         send.start()
 
+    hand_on(W_ORDER[2])
     on_by_y(W_ORDER[2])
     far_pass(3)
     for i in W_ORDER[3:5]:

time: 32.7 us -> 32.4 us (level)
    pallas_call x1, Pallas kernels: 31.6 us -> 31.3 us  [shards(): pl.pallas_call(kernel, out_shape=jax.ShapeDtypeStruct((out_toks, cols), b...]
where the time goes in v7:
time: 32.4 us; the launch traced here: 32.3 us
  Pallas kernels  31.3 us (97%)
  local copies, waits for them, and re-layouts  0.97 us (3%)
    pallas_call x1, Pallas kernels, shards(): pl.pallas_call(kernel, out_shape=jax.ShapeDtypeStruct((out_toks, cols), b...  31.3 us
    unnamed x1, local copies, waits for them, and re-layouts  0.97 us

profile of v7, /device:TPU:1, one launch (start us, length us, event | category | flops | bytes accessed | tf_op | source)
XLA Modules:
  0.0 32.3 jit_solution(14188565275778855763)
XLA Ops:
  0.0 31.3 %shard_map.55 = bf16[256,2048]{1,0:T(8,128)(2,1)S(1)} custom-call(bf16[512,1024]{1,0:T(8,128)(2,1)} %kv_hbm.1, bf16[512,1024]{1,0:T(8,128)(2,1)} %q_hbm.1, f32[16,512]{1,0:T(8,128)} %bitcast.2, f32[16,512]{1,0:T(8,128)} %bitcast.3, bf16[512,2048]{1,0:T(8,128)(2,1)} %w_hbm.1), custom_call_target="tpu_custom_call" | custom-call | flops 2147483648 | bytes 6291456 | tf_op jit(solution)/shard_map/pallas_call | solution.py:518
  31.3 1.0 %copy.7 = bf16[256,2048]{1,0:T(8,128)(2,1)} copy(bf16[256,2048]{1,0:T(8,128)(2,1)S(1)} %shard_map.55) | data formatting | bytes 2097152

commit v8 on v7

--- a/solution.py
+++ b/solution.py
@@ -221,24 +221,26 @@
             decayed = states[m] * jnp.exp(-wide(dec_t, g, m) * ((SUBS - 1 - row_f) * float(sub_len)))
             s_own[g, m:m + 1, :] = jnp.sum(decayed, axis=0, keepdims=True)
 
-    for g in range(groups // 2):
+    for g in range(4):
         turn_near(g)
         first_pass(g)
     pl.semaphore_wait(barrier, len(partners))
+    for g in range(4, groups):
+        turn_near(g)
+        first_pass(g)
+
+    send_x = remote(s_own, s_x, x_sem.at[0], x_sem.at[1], to_x)
+    send_x.start()
     w_import[W_ORDER[0]].start()
+    w_import[W_ORDER[1]].start()
     far[1][0].start()
     for copy in far[0]:
         copy.start()
     w_sib.start()
-    for g in range(groups // 2, groups):
-        turn_near(g)
-        first_pass(g)
-
-    send_x = remote(s_own, s_x, x_sem.at[0], x_sem.at[1], to_x)
-    send_x.start()
     rest = (far[1][1], far[1][f_dec], far[1][f_res], far[2][0], far[2][1], far[1][f_q], far[2][f_q])
-    for i, copy in zip(W_ORDER[1:], rest):
+    for i in W_ORDER[2:]:
         w_import[i].start()
+    for copy in rest:
         copy.start()
 
     def run_starts(states, coefs, length, *where):

time: 32.4 us -> 32.3 us (level)
  no operation moved by 1% of the time
where the time goes in v8:
time: 32.3 us; the launch traced here: 32.2 us
  Pallas kernels  31.2 us (97%)
  local copies, waits for them, and re-layouts  0.97 us (3%)
    pallas_call x1, Pallas kernels, shards(): pl.pallas_call(kernel, out_shape=jax.ShapeDtypeStruct((out_toks, cols), b...  31.2 us
    unnamed x1, local copies, waits for them, and re-layouts  0.97 us

profile of v8, /device:TPU:1, one launch (start us, length us, event | category | flops | bytes accessed | tf_op | source)
XLA Modules:
  0.0 32.2 jit_solution(6977095339569323212)
XLA Ops:
  0.0 31.2 %shard_map.55 = bf16[256,2048]{1,0:T(8,128)(2,1)S(1)} custom-call(bf16[512,1024]{1,0:T(8,128)(2,1)} %kv_hbm.1, bf16[512,1024]{1,0:T(8,128)(2,1)} %q_hbm.1, f32[16,512]{1,0:T(8,128)} %bitcast.2, f32[16,512]{1,0:T(8,128)} %bitcast.3, bf16[512,2048]{1,0:T(8,128)(2,1)} %w_hbm.1), custom_call_target="tpu_custom_call" | custom-call | flops 2147483648 | bytes 6291456 | tf_op jit(solution)/shard_map/pallas_call | solution.py:520
  31.3 1.0 %copy.7 = bf16[256,2048]{1,0:T(8,128)(2,1)} copy(bf16[256,2048]{1,0:T(8,128)(2,1)S(1)} %shard_map.55) | data formatting | bytes 2097152

commit v9 on v8

--- a/solution.py
+++ b/solution.py
@@ -234,14 +234,14 @@
     w_import[W_ORDER[0]].start()
     w_import[W_ORDER[1]].start()
     far[1][0].start()
-    for copy in far[0]:
-        copy.start()
-    w_sib.start()
     rest = (far[1][1], far[1][f_dec], far[1][f_res], far[2][0], far[2][1], far[1][f_q], far[2][f_q])
     for i in W_ORDER[2:]:
         w_import[i].start()
     for copy in rest:
         copy.start()
+    for copy in far[0]:
+        copy.start()
+    w_sib.start()
 
     def run_starts(states, coefs, length, *where):
         dec_of, _, _, _, once_of, run_of = coefs

time: 32.3 us -> 32.3 us (level)
  no operation moved by 1% of the time
where the time goes in v9:
time: 32.3 us; the launch traced here: 32.2 us
  Pallas kernels  31.2 us (97%)
  local copies, waits for them, and re-layouts  0.97 us (3%)
    pallas_call x1, Pallas kernels, shards(): pl.pallas_call(kernel, out_shape=jax.ShapeDtypeStruct((out_toks, cols), b...  31.2 us
    unnamed x1, local copies, waits for them, and re-layouts  0.97 us

profile of v9, /device:TPU:1, one launch (start us, length us, event | category | flops | bytes accessed | tf_op | source)
XLA Modules:
  0.0 32.2 jit_solution(16502089603207475841)
XLA Ops:
  0.0 31.2 %shard_map.55 = bf16[256,2048]{1,0:T(8,128)(2,1)S(1)} custom-call(bf16[512,1024]{1,0:T(8,128)(2,1)} %kv_hbm.1, bf16[512,1024]{1,0:T(8,128)(2,1)} %q_hbm.1, f32[16,512]{1,0:T(8,128)} %bitcast.2, f32[16,512]{1,0:T(8,128)} %bitcast.3, bf16[512,2048]{1,0:T(8,128)(2,1)} %w_hbm.1), custom_call_target="tpu_custom_call" | custom-call | flops 2147483648 | bytes 6291456 | tf_op jit(solution)/shard_map/pallas_call | solution.py:520
  31.3 1.0 %copy.7 = bf16[256,2048]{1,0:T(8,128)(2,1)} copy(bf16[256,2048]{1,0:T(8,128)(2,1)S(1)} %shard_map.55) | data formatting | bytes 2097152
